TPU v7x, 1024 devices: a whole 4x8x16 slice. The times are simulated.
1024 devices in a mesh: width: 16 (over z), hidden: 16 (over y, core), batch: 4 (over x).
Axes of the slice: x: 4, y: 8, z: 16, core: 2. Of those that a mesh axis runs over, the one named last changes fastest.
Arguments:
- tokens: bfloat16 [64, 2, 16384], P('batch', None, 'width'), may hold values from -40 to 40
- norm_gain: bfloat16 [16384], P('width'), may hold values from 0.5 to 1.5
- w_query: bfloat16 [16384, 16384], P('width', 'hidden'), may hold values from -0.046875 to 0.046875
- key_weight: bfloat16 [16384, 1024], P('width', 'hidden'), may hold values from -0.046875 to 0.046875
- value_weight: bfloat16 [16384, 1024], P('width', 'hidden'), may hold values from -0.046875 to 0.046875
- output_weight: bfloat16 [16384, 16384], P('hidden', 'width'), may hold values from -0.5 to 0.5
- rotated_key_cache: bfloat16 [64, 1024, 1024], P(('batch', 'hidden'), 'width'), may hold values from -64 to 64
- stored_value_cache: bfloat16 [64, 1024, 1024], P(('batch', 'hidden'), 'width'), may hold values from -6 to 6
- lengths: int32 [64], P(('batch', 'hidden')), may hold values from 2 to 1024, as said below
- positions: int32 [64], P(('batch', 'hidden')), may hold values from 0 to 4095
Outputs:
- layer_out: bfloat16 [64, 2, 16384], P(('batch', 'hidden'), None, 'width')
Inputs may be any that keep to these rules, and one draw needn't show every extreme that they name: `lengths`: each row's number of valid cache entries; some row has exactly 1024.
All inputs are finite; a program needn't handle non-finite values.
Results may differ from a plain program's by a relative error of at most 0.011.
Values may be sent and summed in bfloat16 or wider, within the bound.
A program may use at most 64 MiB of HBM per device.

v0:
```python
import math

import jax
import jax.numpy as jnp
from jax import lax
from jax.sharding import PartitionSpec as P

MODEL_DIMENSION = 16384
QUERY_HEADS = 128
KEY_VALUE_HEADS = 8
HEAD_SIZE = 128


def merged(part, axis, combine):
    gathered = jax.tree.map(lambda a: lax.all_gather(a, axis), part)

    def take(source):
        return jax.tree.map(lambda a: lax.dynamic_index_in_dim(a, source, 0, False), gathered)

    return lax.fori_loop(
        1, lax.axis_size(axis), lambda source, state: combine(state, take(source)), take(0)
    )


def rotate(values, step_pos):
    full_shape = values.shape
    head_count = full_shape[-1] // HEAD_SIZE
    split_heads = values.reshape(full_shape[:-1] + (head_count, HEAD_SIZE))
    half_dim = HEAD_SIZE // 2
    freq_index = jnp.arange(half_dim, dtype=jnp.float32)
    frequency = jnp.exp(-math.log(500000.0) * 2.0 * freq_index / HEAD_SIZE)
    angles = step_pos[..., None, None] * frequency
    cosine = jnp.cos(angles)
    sines = jnp.sin(angles)
    leading = split_heads[..., :half_dim]
    trailing = split_heads[..., half_dim:]
    rotated = jnp.concatenate(
        [leading * cosine - trailing * sines, trailing * cosine + leading * sines], axis=-1
    )
    return rotated.reshape(full_shape)


def combine_parts(earlier, later):
    max_one, sum_one, value_one = earlier
    max_two, sum_two, value_two = later
    row_peak = jnp.maximum(max_one, max_two)
    factor_one = jnp.exp(max_one - row_peak)
    factor_two = jnp.exp(max_two - row_peak)
    return (
        row_peak,
        sum_one * factor_one + sum_two * factor_two,
        value_one * factor_one[..., None] + value_two * factor_two[..., None],
    )


def flat_product(block, matrix):
    lead_rows, lead_steps, inner = block.shape
    flat = jnp.dot(
        block.reshape(lead_rows * lead_steps, inner), matrix, preferred_element_type=jnp.float32
    )
    return flat.reshape(lead_rows, lead_steps, matrix.shape[1])


def local(
    tokens,
    norm_gain,
    w_query,
    key_weight,
    value_weight,
    output_weight,
    rotated_key_cache,
    stored_value_cache,
    lengths,
    positions,
):
    local_rows = lengths.shape[0]
    slot_total = rotated_key_cache.shape[1]
    group_width = QUERY_HEADS // KEY_VALUE_HEADS
    score_scale = HEAD_SIZE ** (-0.5)
    slot_offset = lax.axis_index("width") * slot_total
    valid_slots = (slot_offset + jnp.arange(slot_total, dtype=jnp.int32))[None, :] < lengths[
        :, None
    ]
    slot_mask = valid_slots[:, None, None, None, :]
    key_tiles = rotated_key_cache.reshape(local_rows, slot_total, KEY_VALUE_HEADS, HEAD_SIZE)
    value_tiles = stored_value_cache.reshape(local_rows, slot_total, KEY_VALUE_HEADS, HEAD_SIZE)
    gain_row = norm_gain.astype(jnp.float32)
    blank_cache = jnp.zeros((local_rows, 0, KEY_VALUE_HEADS * HEAD_SIZE), jnp.bfloat16)
    decode_steps = tokens.shape[1]
    as_float = tokens.astype(jnp.float32)
    squares = jnp.sum(as_float * as_float, axis=2)
    scaled = (as_float * gain_row).astype(jnp.bfloat16)
    query_part = flat_product(scaled, w_query)
    key_part = flat_product(scaled, key_weight)
    value_part = flat_product(scaled, value_weight)
    squares, query_part, key_part, value_part = lax.psum(
        (squares, query_part, key_part, value_part), "width"
    )
    inverse = lax.rsqrt(squares / MODEL_DIMENSION + 1e-05)[..., None]
    query_rows = lax.all_to_all(
        query_part * inverse, "hidden", split_axis=0, concat_axis=2, tiled=True
    )
    current_keys = lax.all_to_all(
        key_part * inverse, "hidden", split_axis=0, concat_axis=2, tiled=True
    )
    current_values = lax.all_to_all(
        value_part * inverse, "hidden", split_axis=0, concat_axis=2, tiled=True
    )
    step_pos = (positions[:, None] + 0 + jnp.arange(decode_steps, dtype=jnp.int32)[None, :]).astype(
        jnp.float32
    )
    query_rows = rotate(query_rows, step_pos).astype(jnp.bfloat16)
    current_keys = rotate(current_keys, step_pos).astype(jnp.bfloat16)
    current_values = current_values.astype(jnp.bfloat16)
    query_head_split = query_rows.reshape(
        local_rows, decode_steps, KEY_VALUE_HEADS, group_width, HEAD_SIZE
    )
    scores = (
        jnp.einsum(
            "rsgjd,rcgd->rsgjc", query_head_split, key_tiles, preferred_element_type=jnp.float32
        )
        * score_scale
    )
    masked = jnp.where(slot_mask, scores, -1e30)
    block_max = jnp.max(masked, axis=-1)
    weights = jnp.where(slot_mask, jnp.exp(masked - block_max[..., None]), 0.0).astype(jnp.bfloat16)
    block_sum = jnp.sum(weights.astype(jnp.float32), axis=-1)
    weighted = jnp.einsum(
        "rsgjc,rcgd->rsgjd", weights, value_tiles, preferred_element_type=jnp.float32
    )
    block_max, block_sum, weighted = merged(
        (block_max, block_sum, weighted), "width", combine_parts
    )
    gathered_keys = jnp.concatenate([blank_cache, current_keys], axis=1)
    gathered_values = jnp.concatenate([blank_cache, current_values], axis=1)
    appended_count = gathered_keys.shape[1]
    appended_keys = gathered_keys.reshape(local_rows, appended_count, KEY_VALUE_HEADS, HEAD_SIZE)
    appended_values = gathered_values.reshape(
        local_rows, appended_count, KEY_VALUE_HEADS, HEAD_SIZE
    )
    new_scores = (
        jnp.einsum(
            "rsgjd,rugd->rsgju", query_head_split, appended_keys, preferred_element_type=jnp.float32
        )
        * score_scale
    )
    visible = (
        jnp.arange(appended_count, dtype=jnp.int32)[None, :]
        <= (0 + jnp.arange(decode_steps, dtype=jnp.int32))[:, None]
    )
    visible = visible[None, :, None, None, :]
    new_masked = jnp.where(visible, new_scores, -1e30)
    new_max = jnp.max(new_masked, axis=-1)
    new_weights = jnp.where(visible, jnp.exp(new_masked - new_max[..., None]), 0.0).astype(
        jnp.bfloat16
    )
    new_sum = jnp.sum(new_weights.astype(jnp.float32), axis=-1)
    new_weighted = jnp.einsum(
        "rsgju,rugd->rsgjd", new_weights, appended_values, preferred_element_type=jnp.float32
    )
    row_peak, row_sum, row_value = combine_parts(
        (block_max, block_sum, weighted), (new_max, new_sum, new_weighted)
    )
    attended = (
        (row_value / row_sum[..., None])
        .reshape(local_rows, decode_steps, QUERY_HEADS * HEAD_SIZE)
        .astype(jnp.bfloat16)
    )
    per_head_layout = lax.all_to_all(attended, "hidden", split_axis=2, concat_axis=0, tiled=True)
    out_terms = flat_product(per_head_layout, output_weight)
    return lax.psum_scatter(out_terms, "hidden", scatter_dimension=0, tiled=True).astype(
        jnp.bfloat16
    )


def solution(mesh):
    return jax.shard_map(
        local,
        mesh=mesh,
        in_specs=(
            P("batch", None, "width"),
            P("width"),
            P("width", "hidden"),
            P("width", "hidden"),
            P("width", "hidden"),
            P("hidden", "width"),
            P(("batch", "hidden"), "width", None),
            P(("batch", "hidden"), "width", None),
            P(("batch", "hidden")),
            P(("batch", "hidden")),
        ),
        out_specs=P(("batch", "hidden"), None, "width"),
        check_vma=False,
    )
```

profile of v0, /device:TPU:1, one launch (start us, length us, event | category | flops | bytes accessed | tf_op | source)
XLA Modules:
  0.0 482.9 jit_solution(6608720197556400924)
XLA Ops:
  6.6 0.8 convert_element_type.78
  7.4 1.0 fusion.19
  8.5 1.1 fusion.7
  10.0 56.8 %all-reduce.1 = (f32[16,2]{0,1:T(2,128)S(1)}, f32[16,2,64]{2,0,1:T(8,128)S(1)}, f32[16,2,64]{2,0,1:T(8,128)S(1)}) all-reduce(f32[16,2]{0,1:T(2,128)S(1)} %copy.108, f32[16,2,64]{2,0,1:T(8,128)S(1)} %fusion.22, f32[16,2,64]{2,0,1:T(8,128)S(1)} %fusion.20), channel_id=1, replica_groups=mesh['width'=16,'hidden'=16,'batch'=4] {'width'}, use_global_device_ids=true, to_apply=%region_2.0 | all-reduce | flops 4128 | bytes 33024 | tf_op jit(solution)/shard_map/psum | solution.py:96
  68.1 82.5 %all-reduce.5.cloned.1.call-done = f32[16,2,1024]{2,0,1:T(8,128)} async-done(((f32[16,2,1024]{2,0,1:T(8,128)}), f32[16,2,1024]{2,0,1:T(8,128)}) %all-reduce.5.cloned.1.call-update) | async-done | bytes 131088 | tf_op jit(solution)/shard_map/psum | solution.py:96
  150.7 1.0 broadcast_multiply_fusion
  151.7 0.7 copy.109
  152.4 16.7 %all-to-all-start = ((f32[16,2,1024]{2,1,0:T(2,128)}), f32[16,2,1024]{2,1,0:T(2,128)S(1)}, u32[]{:S(2)}, u32[]{:S(2)}) async-start(f32[16,2,1024]{2,1,0:T(2,128)} %copy.109), calls=%async_computation | async-start | bytes 262144 | tf_op jit(solution)/shard_map/all_to_all | solution.py:100
  169.3 8.9 %all-to-all-done = f32[16,2,1024]{2,1,0:T(2,128)S(1)} async-done(((f32[16,2,1024]{2,1,0:T(2,128)}), f32[16,2,1024]{2,1,0:T(2,128)S(1)}, u32[]{:S(2)}, u32[]{:S(2)}) %all-to-all-start) | async-done | bytes 131104 | tf_op jit(solution)/shard_map/all_to_all | solution.py:100
  179.0 0.7 copy.116
  179.8 0.6 copy.130
  180.4 3.3 all-to-all-start.2
  183.8 0.7 reshape.289
  184.5 5.9 %all-to-all-done.2 = bf16[16,2,64]{2,1,0:T(2,128)(2,1)S(1)} async-done(((bf16[16,2,64]{2,1,0:T(2,128)(2,1)}), bf16[16,2,64]{2,1,0:T(2,128)(2,1)S(1)}, u32[]{:S(2)}, u32[]{:S(2)}) %all-to-all-start.2) | async-done | bytes 4128 | tf_op jit(solution)/shard_map/all_to_all | solution.py:106
  190.4 3.9 all-to-all-start.1
  194.4 7.0 %all-to-all-done.1 = f32[16,1,128]{2,1,0:T(1,128)S(1)} async-done(((f32[16,1,128]{2,1,0:T(1,128)}), f32[16,1,128]{2,1,0:T(1,128)S(1)}, u32[]{:S(2)}, u32[]{:S(2)}) %all-to-all-start.1) | async-done | bytes 8224 | tf_op jit(solution)/shard_map/all_to_all | solution.py:103
  201.4 0.6 broadcast.115
  202.0 0.7 reduce.4
  203.2 23.6 %all-gather.1 = f32[32,8,16]{2,1,0:T(8,128)S(1)} all-gather(f32[2,8,16]{2,1,0:T(8,128)S(1)} %copy.114), channel_id=3, replica_groups=mesh['width'=16,'hidden'=16,'batch'=4] {'width'}, dimensions={0}, use_global_device_ids=true | all-gather | bytes 17408 | tf_op jit(solution)/shard_map/all_gather | solution.py:15
  226.7 21.5 %all-gather = f32[32,8,16]{2,1,0:T(8,128)S(1)} all-gather(f32[2,8,16]{2,1,0:T(8,128)S(1)} %copy.113), channel_id=2, replica_groups=mesh['width'=16,'hidden'=16,'batch'=4] {'width'}, dimensions={0}, use_global_device_ids=true | all-gather | bytes 17408 | tf_op jit(solution)/shard_map/all_gather | solution.py:15
  248.7 0.9 slice.26
  249.6 17.3 %while.19 = (s32[]{:T(128)}, f32[1,2,8,16]{3,2,1,0:T(8,128)S(1)}, f32[1,2,8,16]{3,2,1,0:T(8,128)S(1)}, f32[1,2,8,16,128]{4,3,2,1,0:T(8,128)S(1)}, f32[16,1,2,8,1...) while((s32[]{:T(128)}, f32[1,2,8,16]{3,2,1,0:T(8,128)S(1)}, ...), condition=%wide.region_6.7_spmd, body=%wide.region_5.6_spmd.sunk | while | flops 100101 | bytes 408731 | solution.py:20
  249.7 1.1 fusion.55
  250.8 1.1 fusion.55
  252.0 1.1 fusion.55
  253.2 1.1 fusion.55
  254.3 1.1 fusion.55
  255.5 1.1 fusion.55
  256.6 1.1 fusion.55
  257.8 1.1 fusion.55
  258.9 1.1 fusion.55
  260.1 1.1 fusion.55
  261.2 1.1 fusion.55
  262.4 1.1 fusion.55
  263.5 1.1 fusion.55
  264.7 1.1 fusion.55
  265.8 1.1 fusion.55
  267.2 12.9 %copy.135 = bf16[1,2,16384]{1,0,2:T(2,128)(2,1)} copy(bf16[1,2,16384]{2,1,0:T(2,128)(2,1)S(1)} %convert_element_type.91) | data formatting | bytes 131072 | tf_op jit(solution)/shard_map/convert_element_type | solution.py:167
  280.6 90.8 %reduce.5 = bf16[16384,2]{1,0:T(8,128)(2,1)} reduce(bf16[16384,1,2]{2,1,0:T(2,128)(2,1)} %bitcast.178, bf16[]{:T(256)} %broadcast.116), dimensions={1}, to_apply=%bitcast.163.reduce_sub_computation | reduce | bytes 131074
  371.4 7.8 %reshape.291 = bf16[16,2,1024]{2,1,0:T(2,128)(2,1)} reshape(bf16[16384,2]{1,0:T(8,128)(2,1)} %reduce.5) | data formatting | bytes 131072
  379.2 15.0 %all-to-all-start.3 = ((bf16[16,2,1024]{2,1,0:T(2,128)(2,1)}), bf16[16,2,1024]{2,1,0:T(2,128)(2,1)S(1)}, u32[]{:S(2)}, u32[]{:S(2)}) async-start(bf16[16,2,1024]{2,1,0:T(2,128)(2,1)} %reshape.291), calls=%async_computation.3 | async-start | bytes 131072 | tf_op jit(solution)/shard_map/all_to_all | solution.py:169
  394.2 1.3 dynamic-slice
  395.5 6.6 %all-to-all-done.3 = bf16[16,2,1024]{2,1,0:T(2,128)(2,1)S(1)} async-done(((bf16[16,2,1024]{2,1,0:T(2,128)(2,1)}), bf16[16,2,1024]{2,1,0:T(2,128)(2,1)S(1)}, u32[]{:S(2)}, u32[]{:S(2)}) %all-to-all-start.3) | async-done | bytes 65568 | tf_op jit(solution)/shard_map/all_to_all | solution.py:169
  402.0 11.9 %reshape.292 = bf16[16384,1,2]{2,1,0:T(2,128)(2,1)} reshape(bf16[16,2,1024]{2,1,0:T(2,128)(2,1)S(1)} %all-to-all-done.3) | data formatting | bytes 131072
  413.9 15.3 %copy.136 = bf16[1,2,16384]{2,1,0:T(2,128)(2,1)S(1)} copy(bf16[1,2,16384]{1,0,2:T(2,128)(2,1)} %bitcast.179) | data formatting | bytes 131072 | tf_op jit(solution)/shard_map/all_to_all | solution.py:169
  429.3 2.1 fusion.5
  431.4 43.4 %all-reduce.6 = bf16[16,2,1024]{2,1,0:T(2,128)(2,1)S(1)} all-reduce(f32[16,2,1024]{2,1,0:T(2,128)S(1)} %copy.137), channel_id=5, replica_groups=mesh['width'=16,'hidden'=16,'batch'=4] {'hidden'}, use_global_device_ids=true, to_apply=%region_11.12.clone | all-reduce | flops 32768 | bytes 196608
  474.8 1.2 dynamic-slice_convert_fusion
  (100 shorter events, 4.1 us)
Async XLA Ops:
  6.5 1.9 copy-start
  6.5 3.1 copy-start.3
  6.5 3.2 copy-start.4
  6.5 162.6 %copy-start.1 = (bf16[1,64,1024]{2,1,0:T(8,128)(2,1)S(1)}, bf16[1,64,1024]{2,1,0:T(8,128)(2,1)}, u32[]{:S(2)}) copy-start(bf16[1,64,1024]{2,1,0:T(8,128)(2,1)} %param.18) | copy-start | bytes 393220
  6.5 162.6 %copy-start.2 = (bf16[1,64,1024]{2,1,0:T(8,128)(2,1)S(1)}, bf16[1,64,1024]{2,1,0:T(8,128)(2,1)}, u32[]{:S(2)}) copy-start(bf16[1,64,1024]{2,1,0:T(8,128)(2,1)} %param.19) | copy-start | bytes 393220
  6.5 144.1 %all-reduce.5.cloned.1.call-start = ((), (), s32[]{:S(2)}) async-start(), calls=%async_computation.4 | async-start | bytes 262144 | tf_op jit(solution)/shard_map/psum | solution.py:96
  152.4 25.8 %all-to-all-start = ((f32[16,2,1024]{2,1,0:T(2,128)}), f32[16,2,1024]{2,1,0:T(2,128)S(1)}, u32[]{:S(2)}, u32[]{:S(2)}) async-start(f32[16,2,1024]{2,1,0:T(2,128)} %copy.109), calls=%async_computation | async-start | bytes 262144 | tf_op jit(solution)/shard_map/all_to_all | solution.py:100
  169.1 79.7 %all-gather.5.cloned.1.call-start = ((), (), s32[]{:S(2)}) async-start(), calls=%async_computation.5 | async-start | bytes 2228224 | tf_op jit(solution)/shard_map/all_gather | solution.py:15
  180.4 10.0 %all-to-all-start.2 = ((bf16[16,2,64]{2,1,0:T(2,128)(2,1)}), bf16[16,2,64]{2,1,0:T(2,128)(2,1)S(1)}, u32[]{:S(2)}, u32[]{:S(2)}) async-start(bf16[16,2,64]{2,1,0:T(2,128)(2,1)} %copy.130), calls=%async_computation.2 | async-start | bytes 16384 | tf_op jit(solution)/shard_map/all_to_all | solution.py:106
  190.4 11.0 %all-to-all-start.1 = ((f32[16,1,128]{2,1,0:T(1,128)}), f32[16,1,128]{2,1,0:T(1,128)S(1)}, u32[]{:S(2)}, u32[]{:S(2)}) async-start(f32[16,1,128]{2,1,0:T(1,128)} %reshape.289), calls=%async_computation.1 | async-start | bytes 16384 | tf_op jit(solution)/shard_map/all_to_all | solution.py:103
  379.2 22.9 %all-to-all-start.3 = ((bf16[16,2,1024]{2,1,0:T(2,128)(2,1)}), bf16[16,2,1024]{2,1,0:T(2,128)(2,1)S(1)}, u32[]{:S(2)}, u32[]{:S(2)}) async-start(bf16[16,2,1024]{2,1,0:T(2,128)(2,1)} %reshape.291), calls=%async_computation.3 | async-start | bytes 131072 | tf_op jit(solution)/shard_map/all_to_all | solution.py:169
Sparse Core Ops, SparseCore 0:
  9.7 140.9 all-reduce.4
  179.8 60.1 all-gather.4
where the time goes:
time: 486 us; the launch traced here: 483 us
  blocking collectives  145 us (30%)
  other arithmetic  112 us (23%)
  waiting for transfers between devices  111 us (23%)
  local copies, waits for them, and re-layouts  55.8 us (11%)
  starting transfers between devices  39 us (8%)
  between operations  14.9 us (3%)
    unnamed x1, other arithmetic  90.8 us
    psum x1, waiting for transfers between devices, local(): lax.psum((squares, query_part, key_part, value_part), 'width')  82.5 us
    psum x1, blocking collectives, local(): lax.psum((squares, query_part, key_part, value_part), 'width')  56.8 us
    all_gather x2, blocking collectives, merged(): gathered = jax.tree.map(lambda a: lax.all_gather(a, axis), part)  45.1 us
    unnamed x1, blocking collectives  43.4 us
    unnamed x18, local copies, waits for them, and re-layouts  22.3 us
    all_to_all x1, starting transfers between devices, local(): lax.all_to_all(query_part * inverse, 'hidden', split_axis=0, concat_axis=...  16.7 us
    add x15, other arithmetic, combine_parts(): value_one * factor_one[..., None] + value_two * factor_two[..., None]  16.1 us
  transfers between devices with their start and end apart: 6, of which 5 were waited for; matrix products, arithmetic and copies ran while one was open for 1% of the time, Pallas kernels for 0%

commit v1 on v0

v1 whole, which is shorter than its diff:
```python
import functools
import math

import jax
import jax.numpy as jnp
from jax import lax
from jax.experimental import pallas as pl
from jax.experimental.pallas import tpu as pltpu
from jax.sharding import PartitionSpec as P

MESH = pl.DeviceIdType.MESH
MODEL_DIMENSION = 16384
HEAD_SIZE = 128
N = 16
GROUP = 8
STEPS = 2
ROWS = N * STEPS
SLOTS = 64
EXTENDED = 80
NEGATIVE = -1e30


def wait_bytes(ref, sem):
    pltpu.make_async_copy(ref, ref, sem).wait()


def to_messages(wide, message):
    for row in range(N):
        parts = [wide[pl.ds(STEPS * row + t, GROUP, stride=ROWS), :] for t in range(STEPS)]
        message[row] = jnp.concatenate(parts, axis=0).astype(jnp.bfloat16)


def kernel(
    lengths,
    positions,
    tokens_hbm,
    gain_ref,
    w_query_hbm,
    key_hbm,
    value_hbm,
    w_out_hbm,
    key_cache_hbm,
    value_cache_hbm,
    out_ref,
    tokens,
    w_query,
    w_key,
    w_value,
    w_out,
    keys,
    values,
    flat,
    wide,
    message,
    aux,
    part_in,
    aux_in,
    query_out,
    fresh_out,
    query_in,
    fresh_in,
    fresh_rows,
    block_out,
    stat_wide,
    stat_out,
    block_in,
    stat_in,
    coef,
    head_out,
    head_in,
    head_wide,
    total,
    out_in,
    load_sem,
    send_sem,
    recv_sem,
):
    z = lax.axis_index("width")
    h = lax.axis_index("hidden")

    chunk = 256
    loads = [
        pltpu.make_async_copy(tokens_hbm, tokens, load_sem.at[0]),
        pltpu.make_async_copy(key_hbm, w_key, load_sem.at[1]),
        pltpu.make_async_copy(value_hbm, w_value, load_sem.at[2]),
    ]
    for c in range(4):
        cols = pl.ds(c * chunk, chunk)
        loads.append(
            pltpu.make_async_copy(w_query_hbm.at[:, cols], w_query.at[:, cols], load_sem.at[3 + c])
        )
    loads.append(
        pltpu.make_async_copy(key_cache_hbm.at[0], keys.at[pl.ds(0, SLOTS)], load_sem.at[7])
    )
    loads.append(
        pltpu.make_async_copy(value_cache_hbm.at[0], values.at[pl.ds(0, SLOTS)], load_sem.at[8])
    )
    loads.append(pltpu.make_async_copy(w_out_hbm, w_out, load_sem.at[9]))
    for load in loads:
        load.start()

    barrier = pltpu.get_barrier_semaphore()

    def greet(d, carry):
        pl.semaphore_signal(
            barrier, inc=1, device_id={"width": lax.rem(z + d, N)}, device_id_type=MESH
        )
        pl.semaphore_signal(
            barrier, inc=1, device_id={"hidden": lax.rem(h + d, N)}, device_id_type=MESH
        )
        return carry

    lax.fori_loop(1, N, greet, 0)

    loads[0].wait()
    for row in range(N):
        flat[pl.ds(STEPS * row, STEPS), :] = tokens[row].astype(jnp.float32)
    x = flat[...]
    gain = gain_ref[...].astype(jnp.float32).reshape(1, -1)
    squares = jnp.sum(x * x, axis=1, keepdims=True)
    scaled = (x * gain).astype(jnp.bfloat16)
    loads[1].wait()
    loads[2].wait()
    new_key = jnp.dot(scaled, w_key[...], preferred_element_type=jnp.float32)
    new_value = jnp.dot(scaled, w_value[...], preferred_element_type=jnp.float32)
    fresh = jnp.concatenate([new_key, new_value], axis=1)
    odd = lax.rem(h, 2) == 1
    fresh = jnp.where(odd, pltpu.roll(fresh, 64, 1), fresh)
    spread = jnp.broadcast_to(squares, (ROWS, HEAD_SIZE))
    for row in range(N):
        aux[row, 0:2, :] = fresh[STEPS * row : STEPS * row + STEPS, :]
        aux[row, 2:4, :] = spread[STEPS * row : STEPS * row + STEPS, :]
    for c in range(4):
        loads[3 + c].wait()
        part = jnp.dot(
            scaled, w_query[:, c * chunk : (c + 1) * chunk], preferred_element_type=jnp.float32
        )
        wide[pl.ds(2 * c * ROWS, ROWS), :] = part[:, :HEAD_SIZE]
        wide[pl.ds((2 * c + 1) * ROWS, ROWS), :] = part[:, HEAD_SIZE:]
    to_messages(wide, message)

    pl.semaphore_wait(barrier, 2 * (N - 1))

    def send_part(d, carry):
        to = lax.rem(z + d, N)
        pltpu.make_async_remote_copy(
            message.at[to],
            part_in.at[z],
            send_sem.at[0],
            recv_sem.at[0],
            device_id={"width": to},
            device_id_type=MESH,
        ).start()
        pltpu.make_async_remote_copy(
            aux.at[to],
            aux_in.at[z],
            send_sem.at[1],
            recv_sem.at[1],
            device_id={"width": to},
            device_id_type=MESH,
        ).start()
        return carry

    lax.fori_loop(1, N, send_part, 0)
    pltpu.make_async_copy(message.at[z], part_in.at[z], recv_sem.at[0]).start()
    pltpu.make_async_copy(aux.at[z], aux_in.at[z], recv_sem.at[1]).start()

    lane = lax.broadcasted_iota(jnp.int32, (STEPS, HEAD_SIZE), 1)
    step = lax.broadcasted_iota(jnp.int32, (STEPS, HEAD_SIZE), 0)
    index = jnp.where(lane < 64, lane, lane - 64).astype(jnp.float32)
    frequency = jnp.exp(-math.log(500000.0) * 2.0 * index / HEAD_SIZE)
    angles = (positions[0] + step).astype(jnp.float32) * frequency
    cosine = jnp.cos(angles)
    sine = jnp.where(lane < 64, -jnp.sin(angles), jnp.sin(angles))
    fresh_rows[...] = jnp.zeros_like(fresh_rows)

    wait_bytes(aux_in, recv_sem.at[1])
    wait_bytes(part_in, recv_sem.at[0])
    summed = jnp.sum(aux_in[...], axis=0)
    inverse = lax.rsqrt(summed[2:4] / MODEL_DIMENSION + 1e-05)
    fresh_out[...] = summed[0:2] * inverse
    q = jnp.sum(part_in[...].astype(jnp.float32), axis=0)
    both = jnp.concatenate(
        [jnp.broadcast_to(inverse[t : t + 1], (GROUP, HEAD_SIZE)) for t in range(STEPS)], axis=0
    )
    query_out[...] = (q * both).astype(jnp.bfloat16)

    def broadcast_row(source, target, index):
        def send(d, carry):
            pltpu.make_async_remote_copy(
                source,
                target.at[h],
                send_sem.at[index],
                recv_sem.at[index],
                device_id={"width": lax.rem(z + d, N), "hidden": z},
                device_id_type=MESH,
            ).start()
            return carry

        lax.fori_loop(1, N, send, 0)

        @pl.when(h == z)
        def _():
            pltpu.make_async_copy(source, target.at[h], recv_sem.at[index]).start()

        @pl.when(h != z)
        def _():
            pltpu.make_async_remote_copy(
                source,
                target.at[h],
                send_sem.at[index],
                recv_sem.at[index],
                device_id={"hidden": z},
                device_id_type=MESH,
            ).start()

    @pl.when(h == z)
    def _():
        pltpu.make_async_copy(fresh_out, fresh_in.at[h], recv_sem.at[3]).start()

    @pl.when(h != z)
    def _():
        pltpu.make_async_remote_copy(
            fresh_out,
            fresh_in.at[h],
            send_sem.at[3],
            recv_sem.at[3],
            device_id={"hidden": z},
            device_id_type=MESH,
        ).start()

    broadcast_row(query_out, query_in, 2)

    loads[7].wait()
    loads[8].wait()

    @pl.when(h == z)
    def _():
        wait_bytes(fresh_in, recv_sem.at[3])
        low = lane < 64
        for g in range(8):
            even = fresh_in[2 * g]
            odd_half = fresh_in[2 * g + 1]
            key = jnp.where(low, even, odd_half)
            value = pltpu.roll(jnp.where(low, odd_half, even), 64, 1)
            key = key * cosine + pltpu.roll(key, 64, 1) * sine
            fresh_rows[0, 0:2, g * 128 : (g + 1) * 128] = key
            fresh_rows[1, 0:2, g * 128 : (g + 1) * 128] = value

    keys[SLOTS:EXTENDED, :] = fresh_rows[0].astype(jnp.bfloat16)
    values[SLOTS:EXTENDED, :] = fresh_rows[1].astype(jnp.bfloat16)

    column = lax.broadcasted_iota(jnp.int32, (2 * N, EXTENDED), 1)
    row_step = lax.rem(lax.broadcasted_iota(jnp.int32, (2 * N, EXTENDED), 0) // GROUP, STEPS)
    here = jnp.where(h == z, 1, 0)
    cached = jnp.where(z * SLOTS + column < lengths[0], 1, 0)
    appended = jnp.where(column - SLOTS <= row_step, here, 0)
    valid = jnp.where(column < SLOTS, cached, appended) == 1
    cosines = jnp.concatenate(
        [jnp.broadcast_to(cosine[t : t + 1], (GROUP, HEAD_SIZE)) for t in (0, 1, 0, 1)], axis=0
    )
    sines = jnp.concatenate(
        [jnp.broadcast_to(sine[t : t + 1], (GROUP, HEAD_SIZE)) for t in (0, 1, 0, 1)], axis=0
    )

    wait_bytes(query_in, recv_sem.at[2])
    for g in range(8):
        cols = slice(g * HEAD_SIZE, (g + 1) * HEAD_SIZE)
        q = jnp.concatenate([query_in[2 * g], query_in[2 * g + 1]], axis=0).astype(jnp.float32)
        q = (q * cosines + pltpu.roll(q, 64, 1) * sines).astype(jnp.bfloat16)
        scores = lax.dot_general(
            q, keys[:, cols], (((1,), (1,)), ((), ())), preferred_element_type=jnp.float32
        ) * (HEAD_SIZE**-0.5)
        masked = jnp.where(valid, scores, NEGATIVE)
        block_max = jnp.max(masked, axis=1, keepdims=True)
        weights = jnp.where(valid, jnp.exp(masked - block_max), 0.0).astype(jnp.bfloat16)
        block_sum = jnp.sum(weights.astype(jnp.float32), axis=1, keepdims=True)
        weighted = jnp.dot(weights, values[:, cols], preferred_element_type=jnp.float32)
        filled = block_sum > 0.0
        safe = jnp.where(filled, block_sum, 1.0)
        level = jnp.where(filled, block_max + jnp.log(safe), NEGATIVE)
        block = (weighted / safe).astype(jnp.bfloat16)
        block_out[2 * g] = block[:N]
        block_out[2 * g + 1] = block[N:]
        stat_wide[2 * g * N : 2 * (g + 1) * N, :] = jnp.broadcast_to(level, (2 * N, HEAD_SIZE))
    for half in range(2):
        turned = stat_wide[half * 128 : (half + 1) * 128, :].T
        stat_out[half] = turned[0:1, :]

    def send_block(d, carry):
        to = lax.rem(z + d, N)
        pltpu.make_async_remote_copy(
            stat_out.at[to // GROUP],
            stat_in.at[z],
            send_sem.at[5],
            recv_sem.at[5],
            device_id={"width": to},
            device_id_type=MESH,
        ).start()
        pltpu.make_async_remote_copy(
            block_out.at[to],
            block_in.at[z],
            send_sem.at[4],
            recv_sem.at[4],
            device_id={"width": to},
            device_id_type=MESH,
        ).start()
        return carry

    lax.fori_loop(1, N, send_block, 0)
    pltpu.make_async_copy(stat_out.at[z // GROUP], stat_in.at[z], recv_sem.at[5]).start()
    pltpu.make_async_copy(block_out.at[z], block_in.at[z], recv_sem.at[4]).start()
    coef[...] = jnp.zeros_like(coef)

    wait_bytes(stat_in, recv_sem.at[5])
    levels = [stat_in[i] for i in range(N)]
    peak = functools.reduce(jnp.maximum, levels)
    factors = [jnp.exp(level - peak) for level in levels]
    denominator = functools.reduce(jnp.add, factors)
    for i in range(N):
        coef[i : i + 1, :] = factors[i] / denominator
    coef[...] = coef[...].T
    mine = coef[pl.ds(pl.multiple_of(lax.rem(z, GROUP) * N, N), N), :]
    wait_bytes(block_in, recv_sem.at[4])
    merged = block_in[0].astype(jnp.float32) * mine[:, 0:1]
    for i in range(1, N):
        merged = merged + block_in[i].astype(jnp.float32) * mine[:, i : i + 1]
    head_out[...] = merged.astype(jnp.bfloat16)

    broadcast_row(head_out, head_in, 6)
    loads[9].wait()
    wait_bytes(head_in, recv_sem.at[6])
    head_wide[...] = head_in[...].astype(jnp.float32).reshape(N * N, HEAD_SIZE)
    attended = jnp.concatenate(
        [head_wide[pl.ds(j, ROWS, stride=GROUP), :].astype(jnp.bfloat16) for j in range(GROUP)],
        axis=1,
    )
    for c in range(4):
        part = jnp.dot(
            attended, w_out[:, c * chunk : (c + 1) * chunk], preferred_element_type=jnp.float32
        )
        wide[pl.ds(2 * c * ROWS, ROWS), :] = part[:, :HEAD_SIZE]
        wide[pl.ds((2 * c + 1) * ROWS, ROWS), :] = part[:, HEAD_SIZE:]
    wait_bytes(message.at[pl.ds(0, N - 1)], send_sem.at[0])
    to_messages(wide, message)

    def send_out(d, carry):
        to = lax.rem(h + d, N)
        pltpu.make_async_remote_copy(
            message.at[to],
            out_in.at[h],
            send_sem.at[7],
            recv_sem.at[7],
            device_id={"hidden": to},
            device_id_type=MESH,
        ).start()
        return carry

    lax.fori_loop(1, N, send_out, 0)
    pltpu.make_async_copy(message.at[h], out_in.at[h], recv_sem.at[7]).start()

    wait_bytes(aux.at[pl.ds(0, N - 1)], send_sem.at[1])
    wait_bytes(query_in.at[pl.ds(0, N - 1)], send_sem.at[2])
    wait_bytes(block_in.at[pl.ds(0, N - 1)], send_sem.at[4])
    wait_bytes(stat_in.at[pl.ds(0, N - 1)], send_sem.at[5])
    wait_bytes(head_in.at[pl.ds(0, N - 1)], send_sem.at[6])

    @pl.when(h != z)
    def _():
        wait_bytes(query_in.at[0], send_sem.at[2])
        wait_bytes(fresh_in.at[0], send_sem.at[3])
        wait_bytes(head_in.at[0], send_sem.at[6])

    wait_bytes(out_in, recv_sem.at[7])
    total[...] = jnp.sum(out_in[...].astype(jnp.float32), axis=0)
    for c in range(GROUP):
        both_steps = total[pl.ds(c, STEPS, stride=GROUP), :]
        out_ref[0, :, c * HEAD_SIZE : (c + 1) * HEAD_SIZE] = both_steps.astype(jnp.bfloat16)
    wait_bytes(out_in.at[pl.ds(0, N - 1)], send_sem.at[7])


def local(
    tokens,
    norm_gain,
    w_query,
    key_weight,
    value_weight,
    output_weight,
    rotated_key_cache,
    stored_value_cache,
    lengths,
    positions,
):
    smem = pl.BlockSpec(memory_space=pltpu.SMEM)
    vmem = pl.BlockSpec(memory_space=pltpu.VMEM)
    anywhere = pl.BlockSpec(memory_space=pl.ANY)
    half, full = jnp.bfloat16, jnp.float32
    features = tokens.shape[2]
    columns = w_query.shape[1]
    scratch = [
        pltpu.VMEM(tokens.shape, half),
        pltpu.VMEM(w_query.shape, half),
        pltpu.VMEM(key_weight.shape, half),
        pltpu.VMEM(value_weight.shape, half),
        pltpu.VMEM(output_weight.shape, half),
        pltpu.VMEM((EXTENDED, 1024), half),
        pltpu.VMEM((EXTENDED, 1024), half),
        pltpu.VMEM((ROWS, features), full),
        pltpu.VMEM((GROUP * ROWS, HEAD_SIZE), full),
        pltpu.VMEM((N, N, HEAD_SIZE), half),
        pltpu.VMEM((N, 4, HEAD_SIZE), full),
        pltpu.VMEM((N, N, HEAD_SIZE), half),
        pltpu.VMEM((N, 4, HEAD_SIZE), full),
        pltpu.VMEM((N, HEAD_SIZE), half),
        pltpu.VMEM((STEPS, HEAD_SIZE), full),
        pltpu.VMEM((N, N, HEAD_SIZE), half),
        pltpu.VMEM((N, STEPS, HEAD_SIZE), full),
        pltpu.VMEM((2, N, 1024), full),
        pltpu.VMEM((N, N, HEAD_SIZE), half),
        pltpu.VMEM((N * N, HEAD_SIZE), full),
        pltpu.VMEM((2, 1, HEAD_SIZE), full),
        pltpu.VMEM((N, N, HEAD_SIZE), half),
        pltpu.VMEM((N, 1, HEAD_SIZE), full),
        pltpu.VMEM((HEAD_SIZE, HEAD_SIZE), full),
        pltpu.VMEM((N, HEAD_SIZE), half),
        pltpu.VMEM((N, N, HEAD_SIZE), half),
        pltpu.VMEM((N * N, HEAD_SIZE), full),
        pltpu.VMEM((N, HEAD_SIZE), full),
        pltpu.VMEM((N, N, HEAD_SIZE), half),
        pltpu.SemaphoreType.DMA((10,)),
        pltpu.SemaphoreType.DMA((8,)),
        pltpu.SemaphoreType.DMA((8,)),
    ]
    return pl.pallas_call(
        kernel,
        out_shape=jax.ShapeDtypeStruct((1, STEPS, columns), half),
        in_specs=[smem, smem, anywhere, vmem] + [anywhere] * 6,
        out_specs=vmem,
        scratch_shapes=scratch,
        compiler_params=pltpu.CompilerParams(
            collective_id=0, has_side_effects=True, vmem_limit_bytes=48 * 2**20
        ),
        name="decode_block",
    )(
        lengths,
        positions,
        tokens,
        norm_gain,
        w_query,
        key_weight,
        value_weight,
        output_weight,
        rotated_key_cache,
        stored_value_cache,
    )


def solution(mesh):
    return jax.shard_map(
        local,
        mesh=mesh,
        in_specs=(
            P("batch", None, "width"),
            P("width"),
            P("width", "hidden"),
            P("width", "hidden"),
            P("width", "hidden"),
            P("hidden", "width"),
            P(("batch", "hidden"), "width", None),
            P(("batch", "hidden"), "width", None),
            P(("batch", "hidden")),
            P(("batch", "hidden")),
        ),
        out_specs=P(("batch", "hidden"), None, "width"),
        check_vma=False,
    )
```

time: 486 us -> 78 us (0.16)
  blocking collectives: 145 us -> 0 us
  other arithmetic: 112 us -> 0 us
  waiting for transfers between devices: 111 us -> 0 us
  Pallas kernels: 0 us -> 67 us
  local copies, waits for them, and re-layouts: 55.8 us -> 9.25 us
  starting transfers between devices: 39 us -> 0 us
  between operations: 14.9 us -> 1.33 us
    unnamed x1 -> x0, other arithmetic: 90.8 us -> none
    psum x1 -> x0, waiting for transfers between devices: 82.5 us -> none  [local(): lax.psum((squares, query_part, key_part, value_part), 'width')]
    pallas_call x0 -> x1, Pallas kernels: none -> 67 us  [local(): pl.pallas_call(kernel, out_shape=jax.ShapeDtypeStruct((1, STEPS, columns)...]
    psum x1 -> x0, blocking collectives: 56.8 us -> none  [local(): lax.psum((squares, query_part, key_part, value_part), 'width')]
    all_gather x2 -> x0, blocking collectives: 45.1 us -> none  [merged(): gathered = jax.tree.map(lambda a: lax.all_gather(a, axis), part)]
    unnamed x1 -> x0, blocking collectives: 43.4 us -> none
    all_to_all x4 -> x0, starting transfers between devices: 38.9 us -> none  [the longest x1 16.7 us: local(): lax.all_to_all(query_part * inverse, 'hidden', split_axis=0, concat_axis=...]
    all_to_all x4 -> x0, waiting for transfers between devices: 28.3 us -> none  [the longest x1 8.92 us: local(): lax.all_to_all(query_part * inverse, 'hidden', split_axis=0, concat_axis=...]
  transfers between devices with their start and end apart: 6 -> 0, of which waited for: 5 -> 0; matrix products, arithmetic and copies ran while one was open for 1% -> 0% of each run, Pallas kernels for 0% -> 0%
where the time goes in v1:
time: 78 us; the launch traced here: 77.6 us
  Pallas kernels  67 us (86%)
  local copies, waits for them, and re-layouts  9.25 us (12%)
  between operations  1.33 us (2%)
    pallas_call x1, Pallas kernels, local(): pl.pallas_call(kernel, out_shape=jax.ShapeDtypeStruct((1, STEPS, columns)...  67 us
    unnamed x15, local copies, waits for them, and re-layouts  9.25 us

profile of v1, /device:TPU:1, one launch (start us, length us, event | category | flops | bytes accessed | tf_op | source)
XLA Modules:
  0.0 77.6 jit_solution(5642072341499463755)
XLA Ops:
  1.3 1.1 %copy.11.key_hbm = bf16[1024,64]{1,0:T(8,128)(2,1)S(1)} copy(bf16[1024,64]{0,1:T(8,128)(2,1)} %param.13) | data formatting | bytes 262144 | tf_op args[3]
  2.4 1.1 %copy.12.value_hbm = bf16[1024,64]{1,0:T(8,128)(2,1)S(1)} copy(bf16[1024,64]{0,1:T(8,128)(2,1)} %param.14) | data formatting | bytes 262144 | tf_op args[4]
  3.5 0.0 copy-start
  3.5 1.6 %copy-done = bf16[1024,1024]{1,0:T(8,128)(2,1)S(1)} copy-done((bf16[1024,1024]{1,0:T(8,128)(2,1)S(1)}, bf16[1024,1024]{1,0:T(8,128)(2,1)}, u32[]{:S(2)}) %copy-start) | copy-done | bytes 2097176
  5.1 0.0 copy-start.1
  5.1 1.6 %copy-done.1 = bf16[1024,1024]{1,0:T(8,128)(2,1)S(1)} copy-done((bf16[1024,1024]{1,0:T(8,128)(2,1)S(1)}, bf16[1024,1024]{1,0:T(8,128)(2,1)}, u32[]{:S(2)}) %copy-start.1) | copy-done | bytes 2097176
  6.6 0.0 copy-start.2
  6.6 0.9 %copy-done.2 = bf16[1,64,1024]{2,1,0:T(8,128)(2,1)S(1)} copy-done((bf16[1,64,1024]{2,1,0:T(8,128)(2,1)S(1)}, bf16[1,64,1024]{2,1,0:T(8,128)(2,1)}, u32[]{:S(2)}) %copy-start.2) | copy-done | bytes 131096
  7.6 0.0 copy-start.3
  7.6 0.9 %copy-done.3 = bf16[1,64,1024]{2,1,0:T(8,128)(2,1)S(1)} copy-done((bf16[1,64,1024]{2,1,0:T(8,128)(2,1)S(1)}, bf16[1,64,1024]{2,1,0:T(8,128)(2,1)}, u32[]{:S(2)}) %copy-start.3) | copy-done | bytes 131096
  8.5 0.0 copy-start.4
  8.5 0.8 %copy-done.4 = bf16[16,2,1024]{2,1,0:T(2,128)(2,1)S(1)} copy-done((bf16[16,2,1024]{2,1,0:T(2,128)(2,1)S(1)}, bf16[16,2,1024]{2,1,0:T(2,128)(2,1)}, u32[]{:S(2)}) %copy-start.4) | copy-done | bytes 65560
  9.3 0.0 copy-start.5
  9.3 0.7 copy-done.5
  10.0 67.0 %decode_block.1 = bf16[1,2,1024]{2,1,0:T(2,128)(2,1)S(1)} custom-call(s32[1]{0:T(128)S(6)} %copy.14.lengths, s32[1]{0:T(128)S(6)} %copy.15.positions, bf16[16,2,1024]{2,1,0:T(2,128)(2,1)S(1)} %copy-done.4, bf16[1024]{0:T(1024)(128)(2,1)S(1)} %copy-done.5, bf16[1024,1024]{1,0:T(8,128)(2,1)S(1)} %copy-done, bf16[1024,64]{1,0:T(8,128)(2,1)S(1)} %copy.11.key_hbm, ...), custom_call_target="tpu_custom_call" | custom-call | tf_op jit(solution)/shard_map/decode_block/pallas_call | solution.py:434
  77.0 0.6 copy.16
Async XLA Ops:
  3.5 1.6 %copy-start = (bf16[1024,1024]{1,0:T(8,128)(2,1)S(1)}, bf16[1024,1024]{1,0:T(8,128)(2,1)}, u32[]{:S(2)}) copy-start(bf16[1024,1024]{1,0:T(8,128)(2,1)} %w_query_hbm.1) | copy-start | bytes 6291460
  5.1 1.6 %copy-start.1 = (bf16[1024,1024]{1,0:T(8,128)(2,1)S(1)}, bf16[1024,1024]{1,0:T(8,128)(2,1)}, u32[]{:S(2)}) copy-start(bf16[1024,1024]{1,0:T(8,128)(2,1)} %w_out_hbm.1) | copy-start | bytes 6291460
  6.6 0.9 %copy-start.2 = (bf16[1,64,1024]{2,1,0:T(8,128)(2,1)S(1)}, bf16[1,64,1024]{2,1,0:T(8,128)(2,1)}, u32[]{:S(2)}) copy-start(bf16[1,64,1024]{2,1,0:T(8,128)(2,1)} %key_cache_hbm.1) | copy-start | bytes 393220
  7.6 0.9 %copy-start.3 = (bf16[1,64,1024]{2,1,0:T(8,128)(2,1)S(1)}, bf16[1,64,1024]{2,1,0:T(8,128)(2,1)}, u32[]{:S(2)}) copy-start(bf16[1,64,1024]{2,1,0:T(8,128)(2,1)} %value_cache_hbm.1) | copy-start | bytes 393220
  8.5 0.8 %copy-start.4 = (bf16[16,2,1024]{2,1,0:T(2,128)(2,1)S(1)}, bf16[16,2,1024]{2,1,0:T(2,128)(2,1)}, u32[]{:S(2)}) copy-start(bf16[16,2,1024]{2,1,0:T(2,128)(2,1)} %tokens_hbm.1) | copy-start | bytes 196612
  9.3 0.7 copy-start.5

commit v2 on v1

--- a/solution.py
+++ b/solution.py
@@ -24,6 +24,16 @@
     pltpu.make_async_copy(ref, ref, sem).wait()
 
 
+def put(source, target, send, recv, **device):
+    return pltpu.make_async_remote_copy(
+        source, target, send, recv, device_id=device, device_id_type=MESH
+    )
+
+
+def far_first(i):
+    return N // 2 + ((i + 1) // 2) * (2 * lax.rem(i, 2) - 1)
+
+
 def to_messages(wide, message):
     for row in range(N):
         parts = [wide[pl.ds(STEPS * row + t, GROUP, stride=ROWS), :] for t in range(STEPS)]
@@ -34,7 +44,7 @@
     lengths,
     positions,
     tokens_hbm,
-    gain_ref,
+    gain_hbm,
     w_query_hbm,
     key_hbm,
     value_hbm,
@@ -43,6 +53,7 @@
     value_cache_hbm,
     out_ref,
     tokens,
+    gain_ref,
     w_query,
     w_key,
     w_value,
@@ -51,6 +62,8 @@
     values,
     flat,
     wide,
+    table_out,
+    table_in,
     message,
     aux,
     part_in,
@@ -84,6 +97,7 @@
         pltpu.make_async_copy(key_hbm, w_key, load_sem.at[1]),
         pltpu.make_async_copy(value_hbm, w_value, load_sem.at[2]),
     ]
+    load_gain = pltpu.make_async_copy(gain_hbm, gain_ref, load_sem.at[10])
     for c in range(4):
         cols = pl.ds(c * chunk, chunk)
         loads.append(
@@ -96,12 +110,14 @@
         pltpu.make_async_copy(value_cache_hbm.at[0], values.at[pl.ds(0, SLOTS)], load_sem.at[8])
     )
     loads.append(pltpu.make_async_copy(w_out_hbm, w_out, load_sem.at[9]))
+    load_gain.start()
     for load in loads:
         load.start()
 
     barrier = pltpu.get_barrier_semaphore()
 
-    def greet(d, carry):
+    def greet(i, carry):
+        d = far_first(i)
         pl.semaphore_signal(
             barrier, inc=1, device_id={"width": lax.rem(z + d, N)}, device_id_type=MESH
         )
@@ -110,9 +126,22 @@
         )
         return carry
 
-    lax.fori_loop(1, N, greet, 0)
+    lax.fori_loop(0, N - 1, greet, 0)
+
+    lane = lax.broadcasted_iota(jnp.int32, (STEPS, HEAD_SIZE), 1)
+    step = lax.broadcasted_iota(jnp.int32, (STEPS, HEAD_SIZE), 0)
+    index = jnp.where(lane < 64, lane, lane - 64).astype(jnp.float32)
+    frequency = jnp.exp(-math.log(500000.0) * 2.0 * index / HEAD_SIZE)
+    angles = (positions[0] + step).astype(jnp.float32) * frequency
+    cosine = jnp.cos(angles)
+    sine = jnp.where(lane < 64, -jnp.sin(angles), jnp.sin(angles))
+    table_out[0] = cosine
+    table_out[1] = sine
+    fresh_rows[...] = jnp.zeros_like(fresh_rows)
+    coef[...] = jnp.zeros_like(coef)
 
     loads[0].wait()
+    load_gain.wait()
     for row in range(N):
         flat[pl.ds(STEPS * row, STEPS), :] = tokens[row].astype(jnp.float32)
     x = flat[...]
@@ -121,8 +150,9 @@
     scaled = (x * gain).astype(jnp.bfloat16)
     loads[1].wait()
     loads[2].wait()
-    new_key = jnp.dot(scaled, w_key[...], preferred_element_type=jnp.float32)
-    new_value = jnp.dot(scaled, w_value[...], preferred_element_type=jnp.float32)
+    by_rows = (((1,), (1,)), ((), ()))
+    new_key = lax.dot_general(scaled, w_key[...], by_rows, preferred_element_type=jnp.float32)
+    new_value = lax.dot_general(scaled, w_value[...], by_rows, preferred_element_type=jnp.float32)
     fresh = jnp.concatenate([new_key, new_value], axis=1)
     odd = lax.rem(h, 2) == 1
     fresh = jnp.where(odd, pltpu.roll(fresh, 64, 1), fresh)
@@ -141,39 +171,39 @@
 
     pl.semaphore_wait(barrier, 2 * (N - 1))
 
-    def send_part(d, carry):
-        to = lax.rem(z + d, N)
-        pltpu.make_async_remote_copy(
-            message.at[to],
-            part_in.at[z],
-            send_sem.at[0],
-            recv_sem.at[0],
-            device_id={"width": to},
-            device_id_type=MESH,
-        ).start()
-        pltpu.make_async_remote_copy(
-            aux.at[to],
-            aux_in.at[z],
-            send_sem.at[1],
-            recv_sem.at[1],
-            device_id={"width": to},
-            device_id_type=MESH,
-        ).start()
+    @pl.when(h == z)
+    def _():
+        def send_table(i, carry):
+            put(
+                table_out,
+                table_in,
+                send_sem.at[8],
+                recv_sem.at[8],
+                hidden=lax.rem(h + far_first(i), N),
+            ).start()
+            return carry
+
+        lax.fori_loop(0, N - 1, send_table, 0)
+        pltpu.make_async_copy(table_out, table_in, recv_sem.at[8]).start()
+
+    def send_part(i, carry):
+        to = lax.rem(z + far_first(i), N)
+        put(message.at[to], part_in.at[z], send_sem.at[0], recv_sem.at[0], width=to).start()
+        put(aux.at[to], aux_in.at[z], send_sem.at[1], recv_sem.at[1], width=to).start()
         return carry
 
-    lax.fori_loop(1, N, send_part, 0)
+    lax.fori_loop(0, N - 1, send_part, 0)
     pltpu.make_async_copy(message.at[z], part_in.at[z], recv_sem.at[0]).start()
     pltpu.make_async_copy(aux.at[z], aux_in.at[z], recv_sem.at[1]).start()
 
-    lane = lax.broadcasted_iota(jnp.int32, (STEPS, HEAD_SIZE), 1)
-    step = lax.broadcasted_iota(jnp.int32, (STEPS, HEAD_SIZE), 0)
-    index = jnp.where(lane < 64, lane, lane - 64).astype(jnp.float32)
-    frequency = jnp.exp(-math.log(500000.0) * 2.0 * index / HEAD_SIZE)
-    angles = (positions[0] + step).astype(jnp.float32) * frequency
-    cosine = jnp.cos(angles)
-    sine = jnp.where(lane < 64, -jnp.sin(angles), jnp.sin(angles))
-    fresh_rows[...] = jnp.zeros_like(fresh_rows)
-
+    wait_bytes(table_in, recv_sem.at[8])
+    cosines, sines = [
+        jnp.concatenate(
+            [jnp.broadcast_to(table_in[k, t : t + 1], (GROUP, HEAD_SIZE)) for t in range(STEPS)],
+            axis=0,
+        )
+        for k in range(2)
+    ]
     wait_bytes(aux_in, recv_sem.at[1])
     wait_bytes(part_in, recv_sem.at[0])
     summed = jnp.sum(aux_in[...], axis=0)
@@ -183,53 +213,33 @@
     both = jnp.concatenate(
         [jnp.broadcast_to(inverse[t : t + 1], (GROUP, HEAD_SIZE)) for t in range(STEPS)], axis=0
     )
-    query_out[...] = (q * both).astype(jnp.bfloat16)
+    q = q * both
+    query_out[...] = (q * cosines + pltpu.roll(q, 64, 1) * sines).astype(jnp.bfloat16)
 
     def broadcast_row(source, target, index):
-        def send(d, carry):
-            pltpu.make_async_remote_copy(
-                source,
-                target.at[h],
-                send_sem.at[index],
-                recv_sem.at[index],
-                device_id={"width": lax.rem(z + d, N), "hidden": z},
-                device_id_type=MESH,
-            ).start()
+        send, recv = send_sem.at[index], recv_sem.at[index]
+
+        def send_row(i, carry):
+            to = lax.rem(z + far_first(i), N)
+            put(source, target.at[h], send, recv, width=to, hidden=z).start()
             return carry
 
-        lax.fori_loop(1, N, send, 0)
-
+        lax.fori_loop(0, N - 1, send_row, 0)
+        send_one(source, target, index)
+
+    def send_one(source, target, index):
         @pl.when(h == z)
         def _():
             pltpu.make_async_copy(source, target.at[h], recv_sem.at[index]).start()
 
         @pl.when(h != z)
         def _():
-            pltpu.make_async_remote_copy(
-                source,
-                target.at[h],
-                send_sem.at[index],
-                recv_sem.at[index],
-                device_id={"hidden": z},
-                device_id_type=MESH,
+            put(
+                source, target.at[h], send_sem.at[index], recv_sem.at[index], hidden=z
             ).start()
 
-    @pl.when(h == z)
-    def _():
-        pltpu.make_async_copy(fresh_out, fresh_in.at[h], recv_sem.at[3]).start()
-
-    @pl.when(h != z)
-    def _():
-        pltpu.make_async_remote_copy(
-            fresh_out,
-            fresh_in.at[h],
-            send_sem.at[3],
-            recv_sem.at[3],
-            device_id={"hidden": z},
-            device_id_type=MESH,
-        ).start()
-
     broadcast_row(query_out, query_in, 2)
+    send_one(fresh_out, fresh_in, 3)
 
     loads[7].wait()
     loads[8].wait()
@@ -256,20 +266,12 @@
     cached = jnp.where(z * SLOTS + column < lengths[0], 1, 0)
     appended = jnp.where(column - SLOTS <= row_step, here, 0)
     valid = jnp.where(column < SLOTS, cached, appended) == 1
-    cosines = jnp.concatenate(
-        [jnp.broadcast_to(cosine[t : t + 1], (GROUP, HEAD_SIZE)) for t in (0, 1, 0, 1)], axis=0
-    )
-    sines = jnp.concatenate(
-        [jnp.broadcast_to(sine[t : t + 1], (GROUP, HEAD_SIZE)) for t in (0, 1, 0, 1)], axis=0
-    )
-
     wait_bytes(query_in, recv_sem.at[2])
     for g in range(8):
         cols = slice(g * HEAD_SIZE, (g + 1) * HEAD_SIZE)
-        q = jnp.concatenate([query_in[2 * g], query_in[2 * g + 1]], axis=0).astype(jnp.float32)
-        q = (q * cosines + pltpu.roll(q, 64, 1) * sines).astype(jnp.bfloat16)
+        q = jnp.concatenate([query_in[2 * g], query_in[2 * g + 1]], axis=0)
         scores = lax.dot_general(
-            q, keys[:, cols], (((1,), (1,)), ((), ())), preferred_element_type=jnp.float32
+            q, keys[:, cols], by_rows, preferred_element_type=jnp.float32
         ) * (HEAD_SIZE**-0.5)
         masked = jnp.where(valid, scores, NEGATIVE)
         block_max = jnp.max(masked, axis=1, keepdims=True)
@@ -287,30 +289,16 @@
         turned = stat_wide[half * 128 : (half + 1) * 128, :].T
         stat_out[half] = turned[0:1, :]
 
-    def send_block(d, carry):
-        to = lax.rem(z + d, N)
-        pltpu.make_async_remote_copy(
-            stat_out.at[to // GROUP],
-            stat_in.at[z],
-            send_sem.at[5],
-            recv_sem.at[5],
-            device_id={"width": to},
-            device_id_type=MESH,
-        ).start()
-        pltpu.make_async_remote_copy(
-            block_out.at[to],
-            block_in.at[z],
-            send_sem.at[4],
-            recv_sem.at[4],
-            device_id={"width": to},
-            device_id_type=MESH,
-        ).start()
+    def send_block(i, carry):
+        to = lax.rem(z + far_first(i), N)
+        stat = stat_out.at[to // GROUP]
+        put(stat, stat_in.at[z], send_sem.at[5], recv_sem.at[5], width=to).start()
+        put(block_out.at[to], block_in.at[z], send_sem.at[4], recv_sem.at[4], width=to).start()
         return carry
 
-    lax.fori_loop(1, N, send_block, 0)
+    lax.fori_loop(0, N - 1, send_block, 0)
     pltpu.make_async_copy(stat_out.at[z // GROUP], stat_in.at[z], recv_sem.at[5]).start()
     pltpu.make_async_copy(block_out.at[z], block_in.at[z], recv_sem.at[4]).start()
-    coef[...] = jnp.zeros_like(coef)
 
     wait_bytes(stat_in, recv_sem.at[5])
     levels = [stat_in[i] for i in range(N)]
@@ -344,19 +332,12 @@
     wait_bytes(message.at[pl.ds(0, N - 1)], send_sem.at[0])
     to_messages(wide, message)
 
-    def send_out(d, carry):
-        to = lax.rem(h + d, N)
-        pltpu.make_async_remote_copy(
-            message.at[to],
-            out_in.at[h],
-            send_sem.at[7],
-            recv_sem.at[7],
-            device_id={"hidden": to},
-            device_id_type=MESH,
-        ).start()
+    def send_out(i, carry):
+        to = lax.rem(h + far_first(i), N)
+        put(message.at[to], out_in.at[h], send_sem.at[7], recv_sem.at[7], hidden=to).start()
         return carry
 
-    lax.fori_loop(1, N, send_out, 0)
+    lax.fori_loop(0, N - 1, send_out, 0)
     pltpu.make_async_copy(message.at[h], out_in.at[h], recv_sem.at[7]).start()
 
     wait_bytes(aux.at[pl.ds(0, N - 1)], send_sem.at[1])
@@ -364,6 +345,11 @@
     wait_bytes(block_in.at[pl.ds(0, N - 1)], send_sem.at[4])
     wait_bytes(stat_in.at[pl.ds(0, N - 1)], send_sem.at[5])
     wait_bytes(head_in.at[pl.ds(0, N - 1)], send_sem.at[6])
+
+    @pl.when(h == z)
+    def _():
+        for _ in range(N - 1):
+            wait_bytes(table_out, send_sem.at[8])
 
     @pl.when(h != z)
     def _():
@@ -393,20 +379,23 @@
 ):
     smem = pl.BlockSpec(memory_space=pltpu.SMEM)
     vmem = pl.BlockSpec(memory_space=pltpu.VMEM)
-    anywhere = pl.BlockSpec(memory_space=pl.ANY)
+    hbm = pl.BlockSpec(memory_space=pltpu.HBM)
     half, full = jnp.bfloat16, jnp.float32
     features = tokens.shape[2]
     columns = w_query.shape[1]
     scratch = [
         pltpu.VMEM(tokens.shape, half),
+        pltpu.VMEM(norm_gain.shape, half),
         pltpu.VMEM(w_query.shape, half),
-        pltpu.VMEM(key_weight.shape, half),
-        pltpu.VMEM(value_weight.shape, half),
+        pltpu.VMEM(key_weight.shape[::-1], half),
+        pltpu.VMEM(value_weight.shape[::-1], half),
         pltpu.VMEM(output_weight.shape, half),
         pltpu.VMEM((EXTENDED, 1024), half),
         pltpu.VMEM((EXTENDED, 1024), half),
         pltpu.VMEM((ROWS, features), full),
         pltpu.VMEM((GROUP * ROWS, HEAD_SIZE), full),
+        pltpu.VMEM((2, STEPS, HEAD_SIZE), full),
+        pltpu.VMEM((2, STEPS, HEAD_SIZE), full),
         pltpu.VMEM((N, N, HEAD_SIZE), half),
         pltpu.VMEM((N, 4, HEAD_SIZE), full),
         pltpu.VMEM((N, N, HEAD_SIZE), half),
@@ -427,18 +416,18 @@
         pltpu.VMEM((N * N, HEAD_SIZE), full),
         pltpu.VMEM((N, HEAD_SIZE), full),
         pltpu.VMEM((N, N, HEAD_SIZE), half),
-        pltpu.SemaphoreType.DMA((10,)),
-        pltpu.SemaphoreType.DMA((8,)),
-        pltpu.SemaphoreType.DMA((8,)),
+        pltpu.SemaphoreType.DMA((11,)),
+        pltpu.SemaphoreType.DMA((9,)),
+        pltpu.SemaphoreType.DMA((9,)),
     ]
     return pl.pallas_call(
         kernel,
         out_shape=jax.ShapeDtypeStruct((1, STEPS, columns), half),
-        in_specs=[smem, smem, anywhere, vmem] + [anywhere] * 6,
+        in_specs=[smem, smem] + [hbm] * 8,
         out_specs=vmem,
         scratch_shapes=scratch,
         compiler_params=pltpu.CompilerParams(
-            collective_id=0, has_side_effects=True, vmem_limit_bytes=48 * 2**20
+            collective_id=0, has_side_effects=True, vmem_limit_bytes=60 * 2**20
         ),
         name="decode_block",
     )(
@@ -447,8 +436,8 @@
         tokens,
         norm_gain,
         w_query,
-        key_weight,
-        value_weight,
+        key_weight.T,
+        value_weight.T,
         output_weight,
         rotated_key_cache,
         stored_value_cache,

time: 78 us -> 66.4 us (0.85)
  local copies, waits for them, and re-layouts: 9.25 us -> 1.28 us
  Pallas kernels: 67 us -> 63.6 us
    unnamed x15 -> x1, local copies, waits for them, and re-layouts: 9.25 us -> 1.28 us
    pallas_call x1, Pallas kernels: 67 us -> 63.6 us  [local(): pl.pallas_call(kernel, out_shape=jax.ShapeDtypeStruct((1, STEPS, columns)...]
where the time goes in v2:
time: 66.4 us; the launch traced here: 66.2 us
  Pallas kernels  63.6 us (96%)
  between operations  1.3 us (2%)
  local copies, waits for them, and re-layouts  1.28 us (2%)
    pallas_call x1, Pallas kernels, local(): pl.pallas_call(kernel, out_shape=jax.ShapeDtypeStruct((1, STEPS, columns)...  63.6 us

profile of v2, /device:TPU:1, one launch (start us, length us, event | category | flops | bytes accessed | tf_op | source)
XLA Modules:
  0.0 66.2 jit_solution(3485965942632882112)
XLA Ops:
  1.3 63.6 %decode_block.1 = bf16[1,2,1024]{2,1,0:T(2,128)(2,1)} custom-call(s32[1]{0:T(128)S(6)} %copy.12.lengths, s32[1]{0:T(128)S(6)} %copy.13.positions, bf16[16,2,1024]{2,1,0:T(2,128)(2,1)} %tokens_hbm.1, bf16[1024]{0:T(1024)(128)(2,1)} %gain_hbm.1, bf16[1024,1024]{1,0:T(8,128)(2,1)} %w_query_hbm.1, bf16[64,1024]{1,0:T(8,128)(2,1)} %bitcast.2, ...), custom_call_target="tpu_custom_call" | custom-call | tf_op jit(solution)/shard_map/decode_block/pallas_call | solution.py:423
  64.9 1.3 %copy.14 = bf16[1,2,1024]{2,1,0:T(2,128)(2,1)} copy(bf16[1,2,1024]{2,1,0:T(2,128)(2,1)} %decode_block.1) | data formatting | bytes 8192

commit v3 on v2

--- a/solution.py
+++ b/solution.py
@@ -16,6 +16,9 @@
 STEPS = 2
 ROWS = N * STEPS
 SLOTS = 64
+SUMS = 8
+PAIR = N // SUMS
+FIRST_MERGE = 12
 EXTENDED = 80
 NEGATIVE = -1e30
 
@@ -90,6 +93,9 @@
 ):
     z = lax.axis_index("width")
     h = lax.axis_index("hidden")
+    sums_here = z < SUMS
+    place = lax.rem(z + N - FIRST_MERGE, N)
+    merges_here = place < SUMS
 
     chunk = 256
     loads = [
@@ -116,17 +122,21 @@
 
     barrier = pltpu.get_barrier_semaphore()
 
-    def greet(i, carry):
-        d = far_first(i)
-        pl.semaphore_signal(
-            barrier, inc=1, device_id={"width": lax.rem(z + d, N)}, device_id_type=MESH
-        )
-        pl.semaphore_signal(
-            barrier, inc=1, device_id={"hidden": lax.rem(h + d, N)}, device_id_type=MESH
-        )
+    def greet_width(i, carry):
+        to = lax.rem(z + far_first(i), N)
+        pl.semaphore_signal(barrier, inc=1, device_id={"width": to}, device_id_type=MESH)
         return carry
 
-    lax.fori_loop(0, N - 1, greet, 0)
+    def greet_hidden(i, carry):
+        to = lax.rem(h + far_first(i), N)
+        pl.semaphore_signal(barrier, inc=1, device_id={"hidden": to}, device_id_type=MESH)
+        return carry
+
+    @pl.when(sums_here)
+    def _():
+        lax.fori_loop(0, N - 1, greet_width, 0)
+
+    lax.fori_loop(0, N - 1, greet_hidden, 0)
 
     lane = lax.broadcasted_iota(jnp.int32, (STEPS, HEAD_SIZE), 1)
     step = lax.broadcasted_iota(jnp.int32, (STEPS, HEAD_SIZE), 0)
@@ -169,82 +179,93 @@
         wide[pl.ds((2 * c + 1) * ROWS, ROWS), :] = part[:, HEAD_SIZE:]
     to_messages(wide, message)
 
-    pl.semaphore_wait(barrier, 2 * (N - 1))
-
-    @pl.when(h == z)
-    def _():
+    pl.semaphore_wait(barrier, N - 1 + SUMS - jnp.where(sums_here, 1, 0))
+
+    @pl.when(h // PAIR == z)
+    def _():
+        mine = table_in.at[lax.rem(h, PAIR)]
+
         def send_table(i, carry):
-            put(
-                table_out,
-                table_in,
-                send_sem.at[8],
-                recv_sem.at[8],
-                hidden=lax.rem(h + far_first(i), N),
-            ).start()
+            to = lax.rem(h + far_first(i), N)
+            put(table_out, mine, send_sem.at[8], recv_sem.at[8], hidden=to).start()
             return carry
 
         lax.fori_loop(0, N - 1, send_table, 0)
-        pltpu.make_async_copy(table_out, table_in, recv_sem.at[8]).start()
+        pltpu.make_async_copy(table_out, mine, recv_sem.at[8]).start()
 
     def send_part(i, carry):
         to = lax.rem(z + far_first(i), N)
-        put(message.at[to], part_in.at[z], send_sem.at[0], recv_sem.at[0], width=to).start()
-        put(aux.at[to], aux_in.at[z], send_sem.at[1], recv_sem.at[1], width=to).start()
+
+        @pl.when(to < SUMS)
+        def _():
+            rows = pl.ds(PAIR * to, PAIR)
+            put(message.at[rows], part_in.at[z], send_sem.at[0], recv_sem.at[0], width=to).start()
+            put(aux.at[rows], aux_in.at[z], send_sem.at[1], recv_sem.at[1], width=to).start()
+
         return carry
 
     lax.fori_loop(0, N - 1, send_part, 0)
-    pltpu.make_async_copy(message.at[z], part_in.at[z], recv_sem.at[0]).start()
-    pltpu.make_async_copy(aux.at[z], aux_in.at[z], recv_sem.at[1]).start()
-
-    wait_bytes(table_in, recv_sem.at[8])
-    cosines, sines = [
-        jnp.concatenate(
-            [jnp.broadcast_to(table_in[k, t : t + 1], (GROUP, HEAD_SIZE)) for t in range(STEPS)],
-            axis=0,
-        )
-        for k in range(2)
-    ]
-    wait_bytes(aux_in, recv_sem.at[1])
-    wait_bytes(part_in, recv_sem.at[0])
-    summed = jnp.sum(aux_in[...], axis=0)
-    inverse = lax.rsqrt(summed[2:4] / MODEL_DIMENSION + 1e-05)
-    fresh_out[...] = summed[0:2] * inverse
-    q = jnp.sum(part_in[...].astype(jnp.float32), axis=0)
-    both = jnp.concatenate(
-        [jnp.broadcast_to(inverse[t : t + 1], (GROUP, HEAD_SIZE)) for t in range(STEPS)], axis=0
-    )
-    q = q * both
-    query_out[...] = (q * cosines + pltpu.roll(q, 64, 1) * sines).astype(jnp.bfloat16)
-
-    def broadcast_row(source, target, index):
+
+    def broadcast_pair(source, target, index, where, nearest):
         send, recv = send_sem.at[index], recv_sem.at[index]
 
         def send_row(i, carry):
-            to = lax.rem(z + far_first(i), N)
-            put(source, target.at[h], send, recv, width=to, hidden=z).start()
+            to = i if nearest else lax.rem(z + far_first(i), N)
+            for k in range(PAIR):
+                other = PAIR * where + k
+                here = jnp.logical_and(to == z, other == h)
+
+                @pl.when(here)
+                def _():
+                    pltpu.make_async_copy(source.at[k], target.at[h], recv).start()
+
+                @pl.when(jnp.logical_not(here))
+                def _():
+                    put(source.at[k], target.at[h], send, recv, width=to, hidden=other).start()
+
             return carry
 
-        lax.fori_loop(0, N - 1, send_row, 0)
-        send_one(source, target, index)
-
-    def send_one(source, target, index):
-        @pl.when(h == z)
-        def _():
-            pltpu.make_async_copy(source, target.at[h], recv_sem.at[index]).start()
-
-        @pl.when(h != z)
-        def _():
-            put(
-                source, target.at[h], send_sem.at[index], recv_sem.at[index], hidden=z
-            ).start()
-
-    broadcast_row(query_out, query_in, 2)
-    send_one(fresh_out, fresh_in, 3)
+        lax.fori_loop(0, N, send_row, 0)
+
+    @pl.when(sums_here)
+    def _():
+        rows = pl.ds(PAIR * z, PAIR)
+        pltpu.make_async_copy(message.at[rows], part_in.at[z], recv_sem.at[0]).start()
+        pltpu.make_async_copy(aux.at[rows], aux_in.at[z], recv_sem.at[1]).start()
+        wait_bytes(table_in, recv_sem.at[8])
+        wait_bytes(aux_in, recv_sem.at[1])
+        summed = jnp.sum(aux_in[...], axis=0)
+        wait_bytes(part_in, recv_sem.at[0])
+        sums = jnp.sum(part_in[...].astype(jnp.float32), axis=0)
+        for k in range(PAIR):
+            inverse = lax.rsqrt(summed[k, 2:4] / MODEL_DIMENSION + 1e-05)
+            fresh_out[k] = summed[k, 0:2] * inverse
+            scale, cosines, sines = [
+                jnp.concatenate(
+                    [jnp.broadcast_to(a[t : t + 1], (GROUP, HEAD_SIZE)) for t in range(STEPS)],
+                    axis=0,
+                )
+                for a in (inverse, table_in[k, 0], table_in[k, 1])
+            ]
+            q = sums[k] * scale
+            query_out[k] = (q * cosines + pltpu.roll(q, 64, 1) * sines).astype(jnp.bfloat16)
+        broadcast_pair(query_out, query_in, 2, z, False)
+        for k in range(PAIR):
+            row = PAIR * z + k
+
+            @pl.when(row == h)
+            def _():
+                pltpu.make_async_copy(fresh_out.at[k], fresh_in.at[h], recv_sem.at[3]).start()
+
+            @pl.when(row != h)
+            def _():
+                target = fresh_in.at[h]
+                put(fresh_out.at[k], target, send_sem.at[3], recv_sem.at[3], hidden=row).start()
 
     loads[7].wait()
     loads[8].wait()
 
-    @pl.when(h == z)
+    @pl.when(h // PAIR == z)
     def _():
         wait_bytes(fresh_in, recv_sem.at[3])
         low = lane < 64
@@ -262,22 +283,29 @@
 
     column = lax.broadcasted_iota(jnp.int32, (2 * N, EXTENDED), 1)
     row_step = lax.rem(lax.broadcasted_iota(jnp.int32, (2 * N, EXTENDED), 0) // GROUP, STEPS)
-    here = jnp.where(h == z, 1, 0)
+    here = jnp.where(h // PAIR == z, 1, 0)
     cached = jnp.where(z * SLOTS + column < lengths[0], 1, 0)
     appended = jnp.where(column - SLOTS <= row_step, here, 0)
     valid = jnp.where(column < SLOTS, cached, appended) == 1
     wait_bytes(query_in, recv_sem.at[2])
+    span = [slice(g * HEAD_SIZE, (g + 1) * HEAD_SIZE) for g in range(8)]
+    scores = []
     for g in range(8):
-        cols = slice(g * HEAD_SIZE, (g + 1) * HEAD_SIZE)
         q = jnp.concatenate([query_in[2 * g], query_in[2 * g + 1]], axis=0)
-        scores = lax.dot_general(
-            q, keys[:, cols], by_rows, preferred_element_type=jnp.float32
-        ) * (HEAD_SIZE**-0.5)
-        masked = jnp.where(valid, scores, NEGATIVE)
+        product = lax.dot_general(
+            q, keys[:, span[g]], by_rows, preferred_element_type=jnp.float32
+        )
+        scores.append(product * (HEAD_SIZE**-0.5))
+    soft = []
+    for g in range(8):
+        masked = jnp.where(valid, scores[g], NEGATIVE)
         block_max = jnp.max(masked, axis=1, keepdims=True)
         weights = jnp.where(valid, jnp.exp(masked - block_max), 0.0).astype(jnp.bfloat16)
         block_sum = jnp.sum(weights.astype(jnp.float32), axis=1, keepdims=True)
-        weighted = jnp.dot(weights, values[:, cols], preferred_element_type=jnp.float32)
+        soft.append((block_max, block_sum, weights))
+    for g in range(8):
+        block_max, block_sum, weights = soft[g]
+        weighted = jnp.dot(weights, values[:, span[g]], preferred_element_type=jnp.float32)
         filled = block_sum > 0.0
         safe = jnp.where(filled, block_sum, 1.0)
         level = jnp.where(filled, block_max + jnp.log(safe), NEGATIVE)
@@ -291,31 +319,43 @@
 
     def send_block(i, carry):
         to = lax.rem(z + far_first(i), N)
-        stat = stat_out.at[to // GROUP]
-        put(stat, stat_in.at[z], send_sem.at[5], recv_sem.at[5], width=to).start()
-        put(block_out.at[to], block_in.at[z], send_sem.at[4], recv_sem.at[4], width=to).start()
+        index = lax.rem(to + N - FIRST_MERGE, N)
+
+        @pl.when(index < SUMS)
+        def _():
+            stat = stat_out.at[index // (SUMS // 2)]
+            block = block_out.at[pl.ds(PAIR * index, PAIR)]
+            put(stat, stat_in.at[z], send_sem.at[5], recv_sem.at[5], width=to).start()
+            put(block, block_in.at[z], send_sem.at[4], recv_sem.at[4], width=to).start()
+
         return carry
 
     lax.fori_loop(0, N - 1, send_block, 0)
-    pltpu.make_async_copy(stat_out.at[z // GROUP], stat_in.at[z], recv_sem.at[5]).start()
-    pltpu.make_async_copy(block_out.at[z], block_in.at[z], recv_sem.at[4]).start()
-
-    wait_bytes(stat_in, recv_sem.at[5])
-    levels = [stat_in[i] for i in range(N)]
-    peak = functools.reduce(jnp.maximum, levels)
-    factors = [jnp.exp(level - peak) for level in levels]
-    denominator = functools.reduce(jnp.add, factors)
-    for i in range(N):
-        coef[i : i + 1, :] = factors[i] / denominator
-    coef[...] = coef[...].T
-    mine = coef[pl.ds(pl.multiple_of(lax.rem(z, GROUP) * N, N), N), :]
-    wait_bytes(block_in, recv_sem.at[4])
-    merged = block_in[0].astype(jnp.float32) * mine[:, 0:1]
-    for i in range(1, N):
-        merged = merged + block_in[i].astype(jnp.float32) * mine[:, i : i + 1]
-    head_out[...] = merged.astype(jnp.bfloat16)
-
-    broadcast_row(head_out, head_in, 6)
+
+    @pl.when(merges_here)
+    def _():
+        stat = stat_out.at[place // (SUMS // 2)]
+        block = block_out.at[pl.ds(PAIR * place, PAIR)]
+        pltpu.make_async_copy(stat, stat_in.at[z], recv_sem.at[5]).start()
+        pltpu.make_async_copy(block, block_in.at[z], recv_sem.at[4]).start()
+        wait_bytes(stat_in, recv_sem.at[5])
+        levels = [stat_in[i] for i in range(N)]
+        peak = functools.reduce(jnp.maximum, levels)
+        factors = [jnp.exp(level - peak) for level in levels]
+        denominator = functools.reduce(jnp.add, factors)
+        for i in range(N):
+            coef[i : i + 1, :] = factors[i] / denominator
+        coef[...] = coef[...].T
+        first = PAIR * N * lax.rem(place, SUMS // 2)
+        mine = coef[pl.ds(pl.multiple_of(first, PAIR * N), PAIR * N), :]
+        wait_bytes(block_in, recv_sem.at[4])
+        merged = jnp.zeros((PAIR * N, HEAD_SIZE), jnp.float32)
+        for i in range(N):
+            block = block_in[i].astype(jnp.float32).reshape(PAIR * N, HEAD_SIZE)
+            merged = merged + block * mine[:, i : i + 1]
+        head_out[...] = merged.astype(jnp.bfloat16).reshape(PAIR, N, HEAD_SIZE)
+        broadcast_pair(head_out, head_in, 6, place, True)
+
     loads[9].wait()
     wait_bytes(head_in, recv_sem.at[6])
     head_wide[...] = head_in[...].astype(jnp.float32).reshape(N * N, HEAD_SIZE)
@@ -329,7 +369,16 @@
         )
         wide[pl.ds(2 * c * ROWS, ROWS), :] = part[:, :HEAD_SIZE]
         wide[pl.ds((2 * c + 1) * ROWS, ROWS), :] = part[:, HEAD_SIZE:]
-    wait_bytes(message.at[pl.ds(0, N - 1)], send_sem.at[0])
+    sent_pairs = SUMS - 1
+
+    wait_bytes(part_in.at[pl.ds(0, sent_pairs)], send_sem.at[0])
+    wait_bytes(aux_in.at[pl.ds(0, sent_pairs)], send_sem.at[1])
+
+    @pl.when(jnp.logical_not(sums_here))
+    def _():
+        wait_bytes(part_in.at[0], send_sem.at[0])
+        wait_bytes(aux_in.at[0], send_sem.at[1])
+
     to_messages(wide, message)
 
     def send_out(i, carry):
@@ -340,22 +389,38 @@
     lax.fori_loop(0, N - 1, send_out, 0)
     pltpu.make_async_copy(message.at[h], out_in.at[h], recv_sem.at[7]).start()
 
-    wait_bytes(aux.at[pl.ds(0, N - 1)], send_sem.at[1])
-    wait_bytes(query_in.at[pl.ds(0, N - 1)], send_sem.at[2])
-    wait_bytes(block_in.at[pl.ds(0, N - 1)], send_sem.at[4])
-    wait_bytes(stat_in.at[pl.ds(0, N - 1)], send_sem.at[5])
-    wait_bytes(head_in.at[pl.ds(0, N - 1)], send_sem.at[6])
-
-    @pl.when(h == z)
+    wait_bytes(block_in.at[pl.ds(0, sent_pairs)], send_sem.at[4])
+    wait_bytes(stat_in.at[pl.ds(0, sent_pairs)], send_sem.at[5])
+
+    @pl.when(jnp.logical_not(merges_here))
+    def _():
+        wait_bytes(block_in.at[0], send_sem.at[4])
+        wait_bytes(stat_in.at[0], send_sem.at[5])
+
+    @pl.when(sums_here)
+    def _():
+        wait_bytes(query_in.at[pl.ds(0, N - 1)], send_sem.at[2])
+        wait_bytes(query_in, send_sem.at[2])
+        wait_bytes(fresh_in.at[0], send_sem.at[3])
+
+        @pl.when(h // PAIR != z)
+        def _():
+            wait_bytes(query_in.at[0], send_sem.at[2])
+            wait_bytes(fresh_in.at[0], send_sem.at[3])
+
+    @pl.when(merges_here)
+    def _():
+        wait_bytes(head_in.at[pl.ds(0, N - 1)], send_sem.at[6])
+        wait_bytes(head_in, send_sem.at[6])
+
+        @pl.when(h // PAIR != place)
+        def _():
+            wait_bytes(head_in.at[0], send_sem.at[6])
+
+    @pl.when(h // PAIR == z)
     def _():
         for _ in range(N - 1):
             wait_bytes(table_out, send_sem.at[8])
-
-    @pl.when(h != z)
-    def _():
-        wait_bytes(query_in.at[0], send_sem.at[2])
-        wait_bytes(fresh_in.at[0], send_sem.at[3])
-        wait_bytes(head_in.at[0], send_sem.at[6])
 
     wait_bytes(out_in, recv_sem.at[7])
     total[...] = jnp.sum(out_in[...].astype(jnp.float32), axis=0)
@@ -377,8 +442,8 @@
     lengths,
     positions,
 ):
+    vmem = pl.BlockSpec(memory_space=pltpu.VMEM)
     smem = pl.BlockSpec(memory_space=pltpu.SMEM)
-    vmem = pl.BlockSpec(memory_space=pltpu.VMEM)
     hbm = pl.BlockSpec(memory_space=pltpu.HBM)
     half, full = jnp.bfloat16, jnp.float32
     features = tokens.shape[2]
@@ -395,23 +460,23 @@
         pltpu.VMEM((ROWS, features), full),
         pltpu.VMEM((GROUP * ROWS, HEAD_SIZE), full),
         pltpu.VMEM((2, STEPS, HEAD_SIZE), full),
-        pltpu.VMEM((2, STEPS, HEAD_SIZE), full),
+        pltpu.VMEM((PAIR, 2, STEPS, HEAD_SIZE), full),
         pltpu.VMEM((N, N, HEAD_SIZE), half),
         pltpu.VMEM((N, 4, HEAD_SIZE), full),
-        pltpu.VMEM((N, N, HEAD_SIZE), half),
-        pltpu.VMEM((N, 4, HEAD_SIZE), full),
-        pltpu.VMEM((N, HEAD_SIZE), half),
-        pltpu.VMEM((STEPS, HEAD_SIZE), full),
+        pltpu.VMEM((N, PAIR, N, HEAD_SIZE), half),
+        pltpu.VMEM((N, PAIR, 4, HEAD_SIZE), full),
+        pltpu.VMEM((PAIR, N, HEAD_SIZE), half),
+        pltpu.VMEM((PAIR, STEPS, HEAD_SIZE), full),
         pltpu.VMEM((N, N, HEAD_SIZE), half),
         pltpu.VMEM((N, STEPS, HEAD_SIZE), full),
         pltpu.VMEM((2, N, 1024), full),
         pltpu.VMEM((N, N, HEAD_SIZE), half),
         pltpu.VMEM((N * N, HEAD_SIZE), full),
         pltpu.VMEM((2, 1, HEAD_SIZE), full),
-        pltpu.VMEM((N, N, HEAD_SIZE), half),
+        pltpu.VMEM((N, PAIR, N, HEAD_SIZE), half),
         pltpu.VMEM((N, 1, HEAD_SIZE), full),
         pltpu.VMEM((HEAD_SIZE, HEAD_SIZE), full),
-        pltpu.VMEM((N, HEAD_SIZE), half),
+        pltpu.VMEM((PAIR, N, HEAD_SIZE), half),
         pltpu.VMEM((N, N, HEAD_SIZE), half),
         pltpu.VMEM((N * N, HEAD_SIZE), full),
         pltpu.VMEM((N, HEAD_SIZE), full),

time: 66.4 us -> 69.3 us (1.044)
  Pallas kernels: 63.6 us -> 66.6 us
    pallas_call x1, Pallas kernels: 63.6 us -> 66.6 us  [local(): pl.pallas_call(kernel, out_shape=jax.ShapeDtypeStruct((1, STEPS, columns)...]
where the time goes in v3:
time: 69.3 us; the launch traced here: 69.1 us
  Pallas kernels  66.6 us (96%)
  between operations  1.3 us (2%)
  local copies, waits for them, and re-layouts  1.28 us (2%)
    pallas_call x1, Pallas kernels, local(): pl.pallas_call(kernel, out_shape=jax.ShapeDtypeStruct((1, STEPS, columns)...  66.6 us

profile of v3, /device:TPU:1, one launch (start us, length us, event | category | flops | bytes accessed | tf_op | source)
XLA Modules:
  0.0 69.1 jit_solution(2570436874017077537)
XLA Ops:
  1.3 66.6 %decode_block.1 = bf16[1,2,1024]{2,1,0:T(2,128)(2,1)} custom-call(s32[1]{0:T(128)S(6)} %copy.12.lengths, s32[1]{0:T(128)S(6)} %copy.13.positions, bf16[16,2,1024]{2,1,0:T(2,128)(2,1)} %tokens_hbm.1, bf16[1024]{0:T(1024)(128)(2,1)} %gain_hbm.1, bf16[1024,1024]{1,0:T(8,128)(2,1)} %w_query_hbm.1, bf16[64,1024]{1,0:T(8,128)(2,1)} %bitcast.2, ...), custom_call_target="tpu_custom_call" | custom-call | tf_op jit(solution)/shard_map/decode_block/pallas_call | solution.py:488
  67.9 1.3 %copy.14 = bf16[1,2,1024]{2,1,0:T(2,128)(2,1)} copy(bf16[1,2,1024]{2,1,0:T(2,128)(2,1)} %decode_block.1) | data formatting | bytes 8192

commit v4 on v3

--- a/solution.py
+++ b/solution.py
@@ -16,9 +16,10 @@
 STEPS = 2
 ROWS = N * STEPS
 SLOTS = 64
-SUMS = 8
-PAIR = N // SUMS
-FIRST_MERGE = 12
+SUM_PLACES = 16
+MERGE_PLACES = 14
+FIRST_SUM, FIRST_SUM_EXTRA = 0, 0
+FIRST_MERGE, FIRST_MERGE_EXTRA = 9, 15
 EXTENDED = 80
 NEGATIVE = -1e30
 
@@ -82,6 +83,7 @@
     block_in,
     stat_in,
     coef,
+    turned,
     head_out,
     head_in,
     head_wide,
@@ -93,9 +95,17 @@
 ):
     z = lax.axis_index("width")
     h = lax.axis_index("hidden")
-    sums_here = z < SUMS
-    place = lax.rem(z + N - FIRST_MERGE, N)
-    merges_here = place < SUMS
+
+    def items(place, first, first_extra, places):
+        one = lax.rem(place + N - first, N)
+        two = lax.rem(place + N - first_extra, N)
+        return (one, one < places), (two + places, two < N - places)
+
+    rows_here = items(z, FIRST_SUM, FIRST_SUM_EXTRA, SUM_PLACES)
+    groups_here = items(z, FIRST_MERGE, FIRST_MERGE_EXTRA, MERGE_PLACES)
+    extra_row = h >= SUM_PLACES
+    row_place = lax.rem(jnp.where(extra_row, h - SUM_PLACES + FIRST_SUM_EXTRA, h + FIRST_SUM), N)
+    at_row_place = z == row_place
 
     chunk = 256
     loads = [
@@ -132,10 +142,7 @@
         pl.semaphore_signal(barrier, inc=1, device_id={"hidden": to}, device_id_type=MESH)
         return carry
 
-    @pl.when(sums_here)
-    def _():
-        lax.fori_loop(0, N - 1, greet_width, 0)
-
+    lax.fori_loop(0, N - 1, greet_width, 0)
     lax.fori_loop(0, N - 1, greet_hidden, 0)
 
     lane = lax.broadcasted_iota(jnp.int32, (STEPS, HEAD_SIZE), 1)
@@ -179,95 +186,99 @@
         wide[pl.ds((2 * c + 1) * ROWS, ROWS), :] = part[:, HEAD_SIZE:]
     to_messages(wide, message)
 
-    pl.semaphore_wait(barrier, N - 1 + SUMS - jnp.where(sums_here, 1, 0))
-
-    @pl.when(h // PAIR == z)
-    def _():
-        mine = table_in.at[lax.rem(h, PAIR)]
+    pl.semaphore_wait(barrier, 2 * (N - 1))
+
+    def give_table(item):
+        mine, sem = table_in.at[item], 8 + item
 
         def send_table(i, carry):
             to = lax.rem(h + far_first(i), N)
-            put(table_out, mine, send_sem.at[8], recv_sem.at[8], hidden=to).start()
+            put(table_out, mine, send_sem.at[sem], recv_sem.at[sem], hidden=to).start()
             return carry
 
         lax.fori_loop(0, N - 1, send_table, 0)
-        pltpu.make_async_copy(table_out, mine, recv_sem.at[8]).start()
+        pltpu.make_async_copy(table_out, mine, recv_sem.at[sem]).start()
+
+    pl.when(jnp.logical_and(at_row_place, jnp.logical_not(extra_row)))(lambda: give_table(0))
+    pl.when(jnp.logical_and(at_row_place, extra_row))(lambda: give_table(1))
 
     def send_part(i, carry):
         to = lax.rem(z + far_first(i), N)
-
-        @pl.when(to < SUMS)
-        def _():
-            rows = pl.ds(PAIR * to, PAIR)
-            put(message.at[rows], part_in.at[z], send_sem.at[0], recv_sem.at[0], width=to).start()
-            put(aux.at[rows], aux_in.at[z], send_sem.at[1], recv_sem.at[1], width=to).start()
+        for item, (row, valid) in enumerate(items(to, FIRST_SUM, FIRST_SUM_EXTRA, SUM_PLACES)):
+
+            @pl.when(valid)
+            def _():
+                send, recv = send_sem.at[0], recv_sem.at[2 * item]
+                put(message.at[row], part_in.at[item, z], send, recv, width=to).start()
+                send, recv = send_sem.at[1], recv_sem.at[2 * item + 1]
+                put(aux.at[row], aux_in.at[item, z], send, recv, width=to).start()
 
         return carry
 
     lax.fori_loop(0, N - 1, send_part, 0)
-
-    def broadcast_pair(source, target, index, where, nearest):
-        send, recv = send_sem.at[index], recv_sem.at[index]
-
+    for item, (row, valid) in enumerate(rows_here):
+
+        @pl.when(valid)
+        def _():
+            first, second = recv_sem.at[2 * item], recv_sem.at[2 * item + 1]
+            pltpu.make_async_copy(message.at[row], part_in.at[item, z], first).start()
+            pltpu.make_async_copy(aux.at[row], aux_in.at[item, z], second).start()
+
+
+    def broadcast(source, target, send, recv, item, far):
         def send_row(i, carry):
-            to = i if nearest else lax.rem(z + far_first(i), N)
-            for k in range(PAIR):
-                other = PAIR * where + k
-                here = jnp.logical_and(to == z, other == h)
-
-                @pl.when(here)
-                def _():
-                    pltpu.make_async_copy(source.at[k], target.at[h], recv).start()
-
-                @pl.when(jnp.logical_not(here))
-                def _():
-                    put(source.at[k], target.at[h], send, recv, width=to, hidden=other).start()
+            to = lax.rem(z + far_first(i), N) if far else i
+            here = jnp.logical_and(to == z, item == h)
+
+            @pl.when(here)
+            def _():
+                pltpu.make_async_copy(source, target.at[h], recv).start()
+
+            @pl.when(jnp.logical_not(here))
+            def _():
+                put(source, target.at[h], send, recv, width=to, hidden=item).start()
 
             return carry
 
         lax.fori_loop(0, N, send_row, 0)
 
-    @pl.when(sums_here)
-    def _():
-        rows = pl.ds(PAIR * z, PAIR)
-        pltpu.make_async_copy(message.at[rows], part_in.at[z], recv_sem.at[0]).start()
-        pltpu.make_async_copy(aux.at[rows], aux_in.at[z], recv_sem.at[1]).start()
-        wait_bytes(table_in, recv_sem.at[8])
-        wait_bytes(aux_in, recv_sem.at[1])
-        summed = jnp.sum(aux_in[...], axis=0)
-        wait_bytes(part_in, recv_sem.at[0])
-        sums = jnp.sum(part_in[...].astype(jnp.float32), axis=0)
-        for k in range(PAIR):
-            inverse = lax.rsqrt(summed[k, 2:4] / MODEL_DIMENSION + 1e-05)
-            fresh_out[k] = summed[k, 0:2] * inverse
-            scale, cosines, sines = [
-                jnp.concatenate(
-                    [jnp.broadcast_to(a[t : t + 1], (GROUP, HEAD_SIZE)) for t in range(STEPS)],
-                    axis=0,
-                )
-                for a in (inverse, table_in[k, 0], table_in[k, 1])
-            ]
-            q = sums[k] * scale
-            query_out[k] = (q * cosines + pltpu.roll(q, 64, 1) * sines).astype(jnp.bfloat16)
-        broadcast_pair(query_out, query_in, 2, z, False)
-        for k in range(PAIR):
-            row = PAIR * z + k
-
-            @pl.when(row == h)
-            def _():
-                pltpu.make_async_copy(fresh_out.at[k], fresh_in.at[h], recv_sem.at[3]).start()
-
-            @pl.when(row != h)
-            def _():
-                target = fresh_in.at[h]
-                put(fresh_out.at[k], target, send_sem.at[3], recv_sem.at[3], hidden=row).start()
+    def sum_row(item, row):
+        first, second = recv_sem.at[2 * item], recv_sem.at[2 * item + 1]
+        wait_bytes(table_in.at[item], recv_sem.at[8 + item])
+        wait_bytes(aux_in.at[item], second)
+        summed = jnp.sum(aux_in[item], axis=0)
+        inverse = lax.rsqrt(summed[2:4] / MODEL_DIMENSION + 1e-05)
+        fresh_out[item] = summed[0:2] * inverse
+        scale, cosines, sines = [
+            jnp.concatenate(
+                [jnp.broadcast_to(a[t : t + 1], (GROUP, HEAD_SIZE)) for t in range(STEPS)],
+                axis=0,
+            )
+            for a in (inverse, table_in[item, 0], table_in[item, 1])
+        ]
+        wait_bytes(part_in.at[item], first)
+        q = jnp.sum(part_in[item].astype(jnp.float32), axis=0) * scale
+        query_out[item] = (q * cosines + pltpu.roll(q, 64, 1) * sines).astype(jnp.bfloat16)
+        broadcast(query_out.at[item], query_in, send_sem.at[2], recv_sem.at[4], row, True)
+
+        @pl.when(row == h)
+        def _():
+            pltpu.make_async_copy(fresh_out.at[item], fresh_in.at[h], recv_sem.at[5]).start()
+
+        @pl.when(row != h)
+        def _():
+            target = fresh_in.at[h]
+            put(fresh_out.at[item], target, send_sem.at[3], recv_sem.at[5], hidden=row).start()
+
+    for item, (row, valid) in enumerate(rows_here):
+        pl.when(valid)(functools.partial(sum_row, item, row))
 
     loads[7].wait()
     loads[8].wait()
 
-    @pl.when(h // PAIR == z)
+    @pl.when(at_row_place)
     def _():
-        wait_bytes(fresh_in, recv_sem.at[3])
+        wait_bytes(fresh_in, recv_sem.at[5])
         low = lane < 64
         for g in range(8):
             even = fresh_in[2 * g]
@@ -283,11 +294,11 @@
 
     column = lax.broadcasted_iota(jnp.int32, (2 * N, EXTENDED), 1)
     row_step = lax.rem(lax.broadcasted_iota(jnp.int32, (2 * N, EXTENDED), 0) // GROUP, STEPS)
-    here = jnp.where(h // PAIR == z, 1, 0)
+    here = jnp.where(at_row_place, 1, 0)
     cached = jnp.where(z * SLOTS + column < lengths[0], 1, 0)
     appended = jnp.where(column - SLOTS <= row_step, here, 0)
     valid = jnp.where(column < SLOTS, cached, appended) == 1
-    wait_bytes(query_in, recv_sem.at[2])
+    wait_bytes(query_in, recv_sem.at[4])
     span = [slice(g * HEAD_SIZE, (g + 1) * HEAD_SIZE) for g in range(8)]
     scores = []
     for g in range(8):
@@ -314,47 +325,54 @@
         block_out[2 * g + 1] = block[N:]
         stat_wide[2 * g * N : 2 * (g + 1) * N, :] = jnp.broadcast_to(level, (2 * N, HEAD_SIZE))
     for half in range(2):
-        turned = stat_wide[half * 128 : (half + 1) * 128, :].T
-        stat_out[half] = turned[0:1, :]
+        levels = stat_wide[half * 128 : (half + 1) * 128, :].T
+        stat_out[half] = levels[0:1, :]
 
     def send_block(i, carry):
         to = lax.rem(z + far_first(i), N)
-        index = lax.rem(to + N - FIRST_MERGE, N)
-
-        @pl.when(index < SUMS)
-        def _():
-            stat = stat_out.at[index // (SUMS // 2)]
-            block = block_out.at[pl.ds(PAIR * index, PAIR)]
-            put(stat, stat_in.at[z], send_sem.at[5], recv_sem.at[5], width=to).start()
-            put(block, block_in.at[z], send_sem.at[4], recv_sem.at[4], width=to).start()
+        for item, (group, valid) in enumerate(items(to, FIRST_MERGE, FIRST_MERGE_EXTRA, MERGE_PLACES)):
+
+            @pl.when(valid)
+            def _():
+                stat = stat_out.at[group // GROUP]
+                send, recv = send_sem.at[5], recv_sem.at[10 + 2 * item]
+                put(stat, stat_in.at[item, z], send, recv, width=to).start()
+                send, recv = send_sem.at[4], recv_sem.at[11 + 2 * item]
+                put(block_out.at[group], block_in.at[item, z], send, recv, width=to).start()
 
         return carry
 
     lax.fori_loop(0, N - 1, send_block, 0)
-
-    @pl.when(merges_here)
-    def _():
-        stat = stat_out.at[place // (SUMS // 2)]
-        block = block_out.at[pl.ds(PAIR * place, PAIR)]
-        pltpu.make_async_copy(stat, stat_in.at[z], recv_sem.at[5]).start()
-        pltpu.make_async_copy(block, block_in.at[z], recv_sem.at[4]).start()
-        wait_bytes(stat_in, recv_sem.at[5])
-        levels = [stat_in[i] for i in range(N)]
+    for item, (group, valid) in enumerate(groups_here):
+
+        @pl.when(valid)
+        def _():
+            first, second = recv_sem.at[10 + 2 * item], recv_sem.at[11 + 2 * item]
+            stat = stat_out.at[group // GROUP]
+            pltpu.make_async_copy(stat, stat_in.at[item, z], first).start()
+            pltpu.make_async_copy(block_out.at[group], block_in.at[item, z], second).start()
+
+
+    def merge_group(item, group):
+        first, second = recv_sem.at[10 + 2 * item], recv_sem.at[11 + 2 * item]
+        wait_bytes(stat_in.at[item], first)
+        levels = [stat_in[item, i] for i in range(N)]
         peak = functools.reduce(jnp.maximum, levels)
         factors = [jnp.exp(level - peak) for level in levels]
         denominator = functools.reduce(jnp.add, factors)
         for i in range(N):
             coef[i : i + 1, :] = factors[i] / denominator
-        coef[...] = coef[...].T
-        first = PAIR * N * lax.rem(place, SUMS // 2)
-        mine = coef[pl.ds(pl.multiple_of(first, PAIR * N), PAIR * N), :]
-        wait_bytes(block_in, recv_sem.at[4])
-        merged = jnp.zeros((PAIR * N, HEAD_SIZE), jnp.float32)
-        for i in range(N):
-            block = block_in[i].astype(jnp.float32).reshape(PAIR * N, HEAD_SIZE)
-            merged = merged + block * mine[:, i : i + 1]
-        head_out[...] = merged.astype(jnp.bfloat16).reshape(PAIR, N, HEAD_SIZE)
-        broadcast_pair(head_out, head_in, 6, place, True)
+        turned[...] = coef[...].T
+        mine = turned[pl.ds(pl.multiple_of(lax.rem(group, GROUP) * N, N), N), :]
+        wait_bytes(block_in.at[item], second)
+        merged = block_in[item, 0].astype(jnp.float32) * mine[:, 0:1]
+        for i in range(1, N):
+            merged = merged + block_in[item, i].astype(jnp.float32) * mine[:, i : i + 1]
+        head_out[item] = merged.astype(jnp.bfloat16)
+        broadcast(head_out.at[item], head_in, send_sem.at[6], recv_sem.at[6], group, False)
+
+    for item, (group, valid) in enumerate(groups_here):
+        pl.when(valid)(functools.partial(merge_group, item, group))
 
     loads[9].wait()
     wait_bytes(head_in, recv_sem.at[6])
@@ -369,16 +387,15 @@
         )
         wide[pl.ds(2 * c * ROWS, ROWS), :] = part[:, :HEAD_SIZE]
         wide[pl.ds((2 * c + 1) * ROWS, ROWS), :] = part[:, HEAD_SIZE:]
-    sent_pairs = SUMS - 1
-
-    wait_bytes(part_in.at[pl.ds(0, sent_pairs)], send_sem.at[0])
-    wait_bytes(aux_in.at[pl.ds(0, sent_pairs)], send_sem.at[1])
-
-    @pl.when(jnp.logical_not(sums_here))
-    def _():
-        wait_bytes(part_in.at[0], send_sem.at[0])
-        wait_bytes(aux_in.at[0], send_sem.at[1])
-
+    for _, valid in rows_here:
+
+        @pl.when(jnp.logical_not(valid))
+        def _():
+            wait_bytes(message.at[0], send_sem.at[0])
+            wait_bytes(aux.at[0], send_sem.at[1])
+
+    wait_bytes(message.at[pl.ds(0, N - 2)], send_sem.at[0])
+    wait_bytes(aux.at[pl.ds(0, N - 2)], send_sem.at[1])
     to_messages(wide, message)
 
     def send_out(i, carry):
@@ -389,38 +406,38 @@
     lax.fori_loop(0, N - 1, send_out, 0)
     pltpu.make_async_copy(message.at[h], out_in.at[h], recv_sem.at[7]).start()
 
-    wait_bytes(block_in.at[pl.ds(0, sent_pairs)], send_sem.at[4])
-    wait_bytes(stat_in.at[pl.ds(0, sent_pairs)], send_sem.at[5])
-
-    @pl.when(jnp.logical_not(merges_here))
-    def _():
-        wait_bytes(block_in.at[0], send_sem.at[4])
-        wait_bytes(stat_in.at[0], send_sem.at[5])
-
-    @pl.when(sums_here)
-    def _():
-        wait_bytes(query_in.at[pl.ds(0, N - 1)], send_sem.at[2])
-        wait_bytes(query_in, send_sem.at[2])
-        wait_bytes(fresh_in.at[0], send_sem.at[3])
-
-        @pl.when(h // PAIR != z)
-        def _():
-            wait_bytes(query_in.at[0], send_sem.at[2])
-            wait_bytes(fresh_in.at[0], send_sem.at[3])
-
-    @pl.when(merges_here)
-    def _():
-        wait_bytes(head_in.at[pl.ds(0, N - 1)], send_sem.at[6])
-        wait_bytes(head_in, send_sem.at[6])
-
-        @pl.when(h // PAIR != place)
-        def _():
-            wait_bytes(head_in.at[0], send_sem.at[6])
-
-    @pl.when(h // PAIR == z)
-    def _():
-        for _ in range(N - 1):
-            wait_bytes(table_out, send_sem.at[8])
+    wait_bytes(block_out.at[pl.ds(0, N - 2)], send_sem.at[4])
+    wait_bytes(stat_in.at[0, pl.ds(0, N - 2)], send_sem.at[5])
+    for item in range(2):
+        row, has_row = rows_here[item]
+        group, has_group = groups_here[item]
+
+        @pl.when(has_row)
+        def _():
+            wait_bytes(query_in.at[pl.ds(0, N - 1)], send_sem.at[2])
+
+            @pl.when(row != h)
+            def _():
+                wait_bytes(query_in.at[0], send_sem.at[2])
+                wait_bytes(fresh_in.at[0], send_sem.at[3])
+
+        @pl.when(has_group)
+        def _():
+            wait_bytes(head_in.at[pl.ds(0, N - 1)], send_sem.at[6])
+
+            @pl.when(group != h)
+            def _():
+                wait_bytes(head_in.at[0], send_sem.at[6])
+
+        @pl.when(jnp.logical_not(has_group))
+        def _():
+            wait_bytes(block_out.at[0], send_sem.at[4])
+            wait_bytes(stat_in.at[0, 0], send_sem.at[5])
+
+        @pl.when(jnp.logical_and(at_row_place, extra_row if item else jnp.logical_not(extra_row)))
+        def _():
+            for _ in range(N - 1):
+                wait_bytes(table_out, send_sem.at[8 + item])
 
     wait_bytes(out_in, recv_sem.at[7])
     total[...] = jnp.sum(out_in[...].astype(jnp.float32), axis=0)
@@ -460,34 +477,35 @@
         pltpu.VMEM((ROWS, features), full),
         pltpu.VMEM((GROUP * ROWS, HEAD_SIZE), full),
         pltpu.VMEM((2, STEPS, HEAD_SIZE), full),
-        pltpu.VMEM((PAIR, 2, STEPS, HEAD_SIZE), full),
+        pltpu.VMEM((2, 2, STEPS, HEAD_SIZE), full),
         pltpu.VMEM((N, N, HEAD_SIZE), half),
         pltpu.VMEM((N, 4, HEAD_SIZE), full),
-        pltpu.VMEM((N, PAIR, N, HEAD_SIZE), half),
-        pltpu.VMEM((N, PAIR, 4, HEAD_SIZE), full),
-        pltpu.VMEM((PAIR, N, HEAD_SIZE), half),
-        pltpu.VMEM((PAIR, STEPS, HEAD_SIZE), full),
+        pltpu.VMEM((2, N, N, HEAD_SIZE), half),
+        pltpu.VMEM((2, N, 4, HEAD_SIZE), full),
+        pltpu.VMEM((2, N, HEAD_SIZE), half),
+        pltpu.VMEM((2, STEPS, HEAD_SIZE), full),
         pltpu.VMEM((N, N, HEAD_SIZE), half),
         pltpu.VMEM((N, STEPS, HEAD_SIZE), full),
         pltpu.VMEM((2, N, 1024), full),
         pltpu.VMEM((N, N, HEAD_SIZE), half),
         pltpu.VMEM((N * N, HEAD_SIZE), full),
         pltpu.VMEM((2, 1, HEAD_SIZE), full),
-        pltpu.VMEM((N, PAIR, N, HEAD_SIZE), half),
-        pltpu.VMEM((N, 1, HEAD_SIZE), full),
+        pltpu.VMEM((2, N, N, HEAD_SIZE), half),
+        pltpu.VMEM((2, N, 1, HEAD_SIZE), full),
         pltpu.VMEM((HEAD_SIZE, HEAD_SIZE), full),
-        pltpu.VMEM((PAIR, N, HEAD_SIZE), half),
+        pltpu.VMEM((HEAD_SIZE, HEAD_SIZE), full),
+        pltpu.VMEM((2, N, HEAD_SIZE), half),
         pltpu.VMEM((N, N, HEAD_SIZE), half),
         pltpu.VMEM((N * N, HEAD_SIZE), full),
         pltpu.VMEM((N, HEAD_SIZE), full),
         pltpu.VMEM((N, N, HEAD_SIZE), half),
         pltpu.SemaphoreType.DMA((11,)),
-        pltpu.SemaphoreType.DMA((9,)),
-        pltpu.SemaphoreType.DMA((9,)),
+        pltpu.SemaphoreType.DMA((10,)),
+        pltpu.SemaphoreType.DMA((14,)),
     ]
     return pl.pallas_call(
         kernel,
-        out_shape=jax.ShapeDtypeStruct((1, STEPS, columns), half),
+        out_shape=pltpu.VMEM((1, STEPS, columns), half),
         in_specs=[smem, smem] + [hbm] * 8,
         out_specs=vmem,
         scratch_shapes=scratch,

time: 69.3 us -> 62.6 us (0.903)
  Pallas kernels: 66.6 us -> 60.6 us
    pallas_call x1, Pallas kernels: 66.6 us -> 60.6 us  [local(): pl.pallas_call(kernel, out_shape=pltpu.VMEM((1, STEPS, columns), half), i...]
where the time goes in v4:
time: 62.6 us; the launch traced here: 62.5 us
  Pallas kernels  60.6 us (97%)
  between operations  1.3 us (2%)
    pallas_call x1, Pallas kernels, local(): pl.pallas_call(kernel, out_shape=pltpu.VMEM((1, STEPS, columns), half), i...  60.6 us

profile of v4, /device:TPU:1, one launch (start us, length us, event | category | flops | bytes accessed | tf_op | source)
XLA Modules:
  0.0 62.5 jit_solution(8382809288120064758)
XLA Ops:
  1.3 60.6 %decode_block.1 = bf16[1,2,1024]{2,1,0:T(2,128)(2,1)S(1)} custom-call(s32[1]{0:T(128)S(6)} %copy.13.lengths, s32[1]{0:T(128)S(6)} %copy.14.positions, bf16[16,2,1024]{2,1,0:T(2,128)(2,1)} %tokens_hbm.1, bf16[1024]{0:T(1024)(128)(2,1)} %gain_hbm.1, bf16[1024,1024]{1,0:T(8,128)(2,1)} %w_query_hbm.1, bf16[64,1024]{1,0:T(8,128)(2,1)} %bitcast.2, ...), custom_call_target="tpu_custom_call" | custom-call | tf_op jit(solution)/shard_map/decode_block/pallas_call | solution.py:506
  61.9 0.6 copy.12

commit v5 on v2

--- a/solution.py
+++ b/solution.py
@@ -16,6 +16,7 @@
 STEPS = 2
 ROWS = N * STEPS
 SLOTS = 64
+HALF = N // 2
 EXTENDED = 80
 NEGATIVE = -1e30
 
@@ -32,6 +33,10 @@
 
 def far_first(i):
     return N // 2 + ((i + 1) // 2) * (2 * lax.rem(i, 2) - 1)
+
+
+def mirror(i):
+    return lax.rem(N + 9 - i, N)
 
 
 def to_messages(wide, message):
@@ -79,6 +84,7 @@
     block_in,
     stat_in,
     coef,
+    turned,
     head_out,
     head_in,
     head_wide,
@@ -90,6 +96,9 @@
 ):
     z = lax.axis_index("width")
     h = lax.axis_index("hidden")
+
+    mine = mirror(z)
+    at_row_place = mine == h
 
     chunk = 256
     loads = [
@@ -116,17 +125,18 @@
 
     barrier = pltpu.get_barrier_semaphore()
 
-    def greet(i, carry):
-        d = far_first(i)
-        pl.semaphore_signal(
-            barrier, inc=1, device_id={"width": lax.rem(z + d, N)}, device_id_type=MESH
-        )
-        pl.semaphore_signal(
-            barrier, inc=1, device_id={"hidden": lax.rem(h + d, N)}, device_id_type=MESH
-        )
+    def greet_width(i, carry):
+        to = lax.rem(z + far_first(i), N)
+        pl.semaphore_signal(barrier, inc=1, device_id={"width": to}, device_id_type=MESH)
         return carry
 
-    lax.fori_loop(0, N - 1, greet, 0)
+    def greet_hidden(i, carry):
+        to = lax.rem(h + far_first(i), N)
+        pl.semaphore_signal(barrier, inc=1, device_id={"hidden": to}, device_id_type=MESH)
+        return carry
+
+    lax.fori_loop(0, N - 1, greet_width, 0)
+    lax.fori_loop(0, N - 1, greet_hidden, 0)
 
     lane = lax.broadcasted_iota(jnp.int32, (STEPS, HEAD_SIZE), 1)
     step = lax.broadcasted_iota(jnp.int32, (STEPS, HEAD_SIZE), 0)
@@ -138,7 +148,6 @@
     table_out[0] = cosine
     table_out[1] = sine
     fresh_rows[...] = jnp.zeros_like(fresh_rows)
-    coef[...] = jnp.zeros_like(coef)
 
     loads[0].wait()
     load_gain.wait()
@@ -171,16 +180,11 @@
 
     pl.semaphore_wait(barrier, 2 * (N - 1))
 
-    @pl.when(h == z)
+    @pl.when(at_row_place)
     def _():
         def send_table(i, carry):
-            put(
-                table_out,
-                table_in,
-                send_sem.at[8],
-                recv_sem.at[8],
-                hidden=lax.rem(h + far_first(i), N),
-            ).start()
+            to = lax.rem(h + far_first(i), N)
+            put(table_out, table_in, send_sem.at[8], recv_sem.at[8], hidden=to).start()
             return carry
 
         lax.fori_loop(0, N - 1, send_table, 0)
@@ -188,67 +192,65 @@
 
     def send_part(i, carry):
         to = lax.rem(z + far_first(i), N)
-        put(message.at[to], part_in.at[z], send_sem.at[0], recv_sem.at[0], width=to).start()
-        put(aux.at[to], aux_in.at[z], send_sem.at[1], recv_sem.at[1], width=to).start()
+        row = mirror(to)
+        put(message.at[row], part_in.at[z], send_sem.at[0], recv_sem.at[0], width=to).start()
+        put(aux.at[row], aux_in.at[z], send_sem.at[1], recv_sem.at[1], width=to).start()
         return carry
 
     lax.fori_loop(0, N - 1, send_part, 0)
-    pltpu.make_async_copy(message.at[z], part_in.at[z], recv_sem.at[0]).start()
-    pltpu.make_async_copy(aux.at[z], aux_in.at[z], recv_sem.at[1]).start()
+    pltpu.make_async_copy(message.at[mine], part_in.at[z], recv_sem.at[0]).start()
+    pltpu.make_async_copy(aux.at[mine], aux_in.at[z], recv_sem.at[1]).start()
+
+    def broadcast(source, target, send, recv, farthest):
+        def send_row(i, carry):
+            to = lax.rem(z + far_first(i), N) if farthest else i
+            here = jnp.logical_and(to == z, at_row_place)
+
+            @pl.when(here)
+            def _():
+                pltpu.make_async_copy(source, target.at[h], recv).start()
+
+            @pl.when(jnp.logical_not(here))
+            def _():
+                put(source, target.at[h], send, recv, width=to, hidden=mine).start()
+
+            return carry
+
+        lax.fori_loop(0, N, send_row, 0)
 
     wait_bytes(table_in, recv_sem.at[8])
-    cosines, sines = [
-        jnp.concatenate(
-            [jnp.broadcast_to(table_in[k, t : t + 1], (GROUP, HEAD_SIZE)) for t in range(STEPS)],
-            axis=0,
-        )
-        for k in range(2)
-    ]
     wait_bytes(aux_in, recv_sem.at[1])
-    wait_bytes(part_in, recv_sem.at[0])
     summed = jnp.sum(aux_in[...], axis=0)
     inverse = lax.rsqrt(summed[2:4] / MODEL_DIMENSION + 1e-05)
     fresh_out[...] = summed[0:2] * inverse
-    q = jnp.sum(part_in[...].astype(jnp.float32), axis=0)
-    both = jnp.concatenate(
-        [jnp.broadcast_to(inverse[t : t + 1], (GROUP, HEAD_SIZE)) for t in range(STEPS)], axis=0
-    )
-    q = q * both
+    scale, cosines, sines = [
+        jnp.concatenate(
+            [jnp.broadcast_to(a[t : t + 1], (GROUP, HEAD_SIZE)) for t in range(STEPS)], axis=0
+        )
+        for a in (inverse, table_in[0], table_in[1])
+    ]
+    wait_bytes(part_in, recv_sem.at[0])
+    q = jnp.sum(part_in[...].astype(jnp.float32), axis=0) * scale
     query_out[...] = (q * cosines + pltpu.roll(q, 64, 1) * sines).astype(jnp.bfloat16)
-
-    def broadcast_row(source, target, index):
-        send, recv = send_sem.at[index], recv_sem.at[index]
-
-        def send_row(i, carry):
-            to = lax.rem(z + far_first(i), N)
-            put(source, target.at[h], send, recv, width=to, hidden=z).start()
-            return carry
-
-        lax.fori_loop(0, N - 1, send_row, 0)
-        send_one(source, target, index)
-
-    def send_one(source, target, index):
-        @pl.when(h == z)
-        def _():
-            pltpu.make_async_copy(source, target.at[h], recv_sem.at[index]).start()
-
-        @pl.when(h != z)
-        def _():
-            put(
-                source, target.at[h], send_sem.at[index], recv_sem.at[index], hidden=z
-            ).start()
-
-    broadcast_row(query_out, query_in, 2)
-    send_one(fresh_out, fresh_in, 3)
+    batch = lax.rem(h + 2, N) // HALF
+    @pl.when(at_row_place)
+    def _():
+        pltpu.make_async_copy(fresh_out, fresh_in.at[h], recv_sem.at[4 + batch]).start()
+
+    @pl.when(jnp.logical_not(at_row_place))
+    def _():
+        recv = recv_sem.at[4 + batch]
+        put(fresh_out, fresh_in.at[h], send_sem.at[3], recv, hidden=mine).start()
+
+    broadcast(query_out, query_in, send_sem.at[2], recv_sem.at[2 + batch], True)
 
     loads[7].wait()
     loads[8].wait()
-
-    @pl.when(h == z)
-    def _():
-        wait_bytes(fresh_in, recv_sem.at[3])
-        low = lane < 64
-        for g in range(8):
+    low = lane < 64
+
+    def take_fresh(half, heads):
+        wait_bytes(fresh_in.at[pl.ds(0, HALF)], recv_sem.at[4 + half])
+        for g in heads:
             even = fresh_in[2 * g]
             odd_half = fresh_in[2 * g + 1]
             key = jnp.where(low, even, odd_half)
@@ -256,66 +258,87 @@
             key = key * cosine + pltpu.roll(key, 64, 1) * sine
             fresh_rows[0, 0:2, g * 128 : (g + 1) * 128] = key
             fresh_rows[1, 0:2, g * 128 : (g + 1) * 128] = value
+            cols = slice(g * HEAD_SIZE, (g + 1) * HEAD_SIZE)
+            keys[SLOTS:EXTENDED, cols] = fresh_rows[0, :, cols].astype(jnp.bfloat16)
+            values[SLOTS:EXTENDED, cols] = fresh_rows[1, :, cols].astype(jnp.bfloat16)
 
     keys[SLOTS:EXTENDED, :] = fresh_rows[0].astype(jnp.bfloat16)
     values[SLOTS:EXTENDED, :] = fresh_rows[1].astype(jnp.bfloat16)
 
     column = lax.broadcasted_iota(jnp.int32, (2 * N, EXTENDED), 1)
     row_step = lax.rem(lax.broadcasted_iota(jnp.int32, (2 * N, EXTENDED), 0) // GROUP, STEPS)
-    here = jnp.where(h == z, 1, 0)
+    here = jnp.where(at_row_place, 1, 0)
     cached = jnp.where(z * SLOTS + column < lengths[0], 1, 0)
     appended = jnp.where(column - SLOTS <= row_step, here, 0)
     valid = jnp.where(column < SLOTS, cached, appended) == 1
-    wait_bytes(query_in, recv_sem.at[2])
-    for g in range(8):
-        cols = slice(g * HEAD_SIZE, (g + 1) * HEAD_SIZE)
-        q = jnp.concatenate([query_in[2 * g], query_in[2 * g + 1]], axis=0)
-        scores = lax.dot_general(
-            q, keys[:, cols], by_rows, preferred_element_type=jnp.float32
-        ) * (HEAD_SIZE**-0.5)
-        masked = jnp.where(valid, scores, NEGATIVE)
-        block_max = jnp.max(masked, axis=1, keepdims=True)
-        weights = jnp.where(valid, jnp.exp(masked - block_max), 0.0).astype(jnp.bfloat16)
-        block_sum = jnp.sum(weights.astype(jnp.float32), axis=1, keepdims=True)
-        weighted = jnp.dot(weights, values[:, cols], preferred_element_type=jnp.float32)
-        filled = block_sum > 0.0
-        safe = jnp.where(filled, block_sum, 1.0)
-        level = jnp.where(filled, block_max + jnp.log(safe), NEGATIVE)
-        block = (weighted / safe).astype(jnp.bfloat16)
-        block_out[2 * g] = block[:N]
-        block_out[2 * g + 1] = block[N:]
-        stat_wide[2 * g * N : 2 * (g + 1) * N, :] = jnp.broadcast_to(level, (2 * N, HEAD_SIZE))
-    for half in range(2):
-        turned = stat_wide[half * 128 : (half + 1) * 128, :].T
-        stat_out[half] = turned[0:1, :]
-
-    def send_block(i, carry):
-        to = lax.rem(z + far_first(i), N)
-        stat = stat_out.at[to // GROUP]
-        put(stat, stat_in.at[z], send_sem.at[5], recv_sem.at[5], width=to).start()
-        put(block_out.at[to], block_in.at[z], send_sem.at[4], recv_sem.at[4], width=to).start()
-        return carry
-
-    lax.fori_loop(0, N - 1, send_block, 0)
-    pltpu.make_async_copy(stat_out.at[z // GROUP], stat_in.at[z], recv_sem.at[5]).start()
-    pltpu.make_async_copy(block_out.at[z], block_in.at[z], recv_sem.at[4]).start()
-
-    wait_bytes(stat_in, recv_sem.at[5])
+    span = [slice(g * HEAD_SIZE, (g + 1) * HEAD_SIZE) for g in range(8)]
+    coef[...] = jnp.zeros_like(coef)
+    for half, heads in enumerate(((7, 0, 1, 2), (3, 4, 5, 6))):
+        pl.when(at_row_place)(functools.partial(take_fresh, half, heads))
+        wait_bytes(query_in.at[pl.ds(0, HALF)], recv_sem.at[2 + half])
+        scores = []
+        for g in heads:
+            q = jnp.concatenate([query_in[2 * g], query_in[2 * g + 1]], axis=0)
+            product = lax.dot_general(
+                q, keys[:, span[g]], by_rows, preferred_element_type=jnp.float32
+            )
+            scores.append(product * (HEAD_SIZE**-0.5))
+        soft = []
+        for score in scores:
+            masked = jnp.where(valid, score, NEGATIVE)
+            block_max = jnp.max(masked, axis=1, keepdims=True)
+            weights = jnp.where(valid, jnp.exp(masked - block_max), 0.0).astype(jnp.bfloat16)
+            block_sum = jnp.sum(weights.astype(jnp.float32), axis=1, keepdims=True)
+            soft.append((block_max, block_sum, weights))
+        for i, g in enumerate(heads):
+            block_max, block_sum, weights = soft[i]
+            weighted = jnp.dot(weights, values[:, span[g]], preferred_element_type=jnp.float32)
+            filled = block_sum > 0.0
+            safe = jnp.where(filled, block_sum, 1.0)
+            level = jnp.where(filled, block_max + jnp.log(safe), NEGATIVE)
+            block = (weighted / safe).astype(jnp.bfloat16)
+            block_out[2 * g] = block[:N]
+            block_out[2 * g + 1] = block[N:]
+            stat_wide[2 * i * N : 2 * (i + 1) * N, :] = jnp.broadcast_to(level, (2 * N, HEAD_SIZE))
+        levels = stat_wide[...].T
+        stat_out[half] = levels[0:1, :]
+
+        def send_block(i, carry):
+            to = lax.rem(z + far_first(i), N)
+            group = mirror(to)
+
+            @pl.when(lax.rem(group + 2, N) // HALF == half)
+            def _():
+                send, recv = send_sem.at[5], recv_sem.at[10]
+                put(stat_out.at[half], stat_in.at[z], send, recv, width=to).start()
+                send, recv = send_sem.at[4], recv_sem.at[11]
+                put(block_out.at[group], block_in.at[z], send, recv, width=to).start()
+
+            return carry
+
+        lax.fori_loop(0, N - 1, send_block, 0)
+
+        @pl.when(lax.rem(mine + 2, N) // HALF == half)
+        def _():
+            pltpu.make_async_copy(stat_out.at[half], stat_in.at[z], recv_sem.at[10]).start()
+            pltpu.make_async_copy(block_out.at[mine], block_in.at[z], recv_sem.at[11]).start()
+
+    wait_bytes(stat_in, recv_sem.at[10])
     levels = [stat_in[i] for i in range(N)]
     peak = functools.reduce(jnp.maximum, levels)
     factors = [jnp.exp(level - peak) for level in levels]
     denominator = functools.reduce(jnp.add, factors)
     for i in range(N):
         coef[i : i + 1, :] = factors[i] / denominator
-    coef[...] = coef[...].T
-    mine = coef[pl.ds(pl.multiple_of(lax.rem(z, GROUP) * N, N), N), :]
-    wait_bytes(block_in, recv_sem.at[4])
-    merged = block_in[0].astype(jnp.float32) * mine[:, 0:1]
+    turned[...] = coef[...].T
+    shares = turned[pl.ds(pl.multiple_of(lax.rem(mine + 2, GROUP) * N, N), N), :]
+    wait_bytes(block_in, recv_sem.at[11])
+    merged = block_in[0].astype(jnp.float32) * shares[:, 0:1]
     for i in range(1, N):
-        merged = merged + block_in[i].astype(jnp.float32) * mine[:, i : i + 1]
+        merged = merged + block_in[i].astype(jnp.float32) * shares[:, i : i + 1]
     head_out[...] = merged.astype(jnp.bfloat16)
-
-    broadcast_row(head_out, head_in, 6)
+    broadcast(head_out, head_in, send_sem.at[6], recv_sem.at[6], False)
+
     loads[9].wait()
     wait_bytes(head_in, recv_sem.at[6])
     head_wide[...] = head_in[...].astype(jnp.float32).reshape(N * N, HEAD_SIZE)
@@ -330,32 +353,34 @@
         wide[pl.ds(2 * c * ROWS, ROWS), :] = part[:, :HEAD_SIZE]
         wide[pl.ds((2 * c + 1) * ROWS, ROWS), :] = part[:, HEAD_SIZE:]
     wait_bytes(message.at[pl.ds(0, N - 1)], send_sem.at[0])
+    wait_bytes(aux.at[pl.ds(0, N - 1)], send_sem.at[1])
     to_messages(wide, message)
 
-    def send_out(i, carry):
-        to = lax.rem(h + far_first(i), N)
-        put(message.at[to], out_in.at[h], send_sem.at[7], recv_sem.at[7], hidden=to).start()
+    def send_out(to, carry):
+        @pl.when(to != h)
+        def _():
+            put(message.at[to], out_in.at[h], send_sem.at[7], recv_sem.at[7], hidden=to).start()
+
         return carry
 
-    lax.fori_loop(0, N - 1, send_out, 0)
+    lax.fori_loop(0, N, send_out, 0)
     pltpu.make_async_copy(message.at[h], out_in.at[h], recv_sem.at[7]).start()
 
-    wait_bytes(aux.at[pl.ds(0, N - 1)], send_sem.at[1])
     wait_bytes(query_in.at[pl.ds(0, N - 1)], send_sem.at[2])
     wait_bytes(block_in.at[pl.ds(0, N - 1)], send_sem.at[4])
     wait_bytes(stat_in.at[pl.ds(0, N - 1)], send_sem.at[5])
     wait_bytes(head_in.at[pl.ds(0, N - 1)], send_sem.at[6])
 
-    @pl.when(h == z)
-    def _():
-        for _ in range(N - 1):
-            wait_bytes(table_out, send_sem.at[8])
-
-    @pl.when(h != z)
+    @pl.when(jnp.logical_not(at_row_place))
     def _():
         wait_bytes(query_in.at[0], send_sem.at[2])
         wait_bytes(fresh_in.at[0], send_sem.at[3])
         wait_bytes(head_in.at[0], send_sem.at[6])
+
+    @pl.when(at_row_place)
+    def _():
+        for _ in range(N - 1):
+            wait_bytes(table_out, send_sem.at[8])
 
     wait_bytes(out_in, recv_sem.at[7])
     total[...] = jnp.sum(out_in[...].astype(jnp.float32), axis=0)
@@ -377,8 +402,8 @@
     lengths,
     positions,
 ):
+    vmem = pl.BlockSpec(memory_space=pltpu.VMEM)
     smem = pl.BlockSpec(memory_space=pltpu.SMEM)
-    vmem = pl.BlockSpec(memory_space=pltpu.VMEM)
     hbm = pl.BlockSpec(memory_space=pltpu.HBM)
     half, full = jnp.bfloat16, jnp.float32
     features = tokens.shape[2]
@@ -406,11 +431,12 @@
         pltpu.VMEM((N, STEPS, HEAD_SIZE), full),
         pltpu.VMEM((2, N, 1024), full),
         pltpu.VMEM((N, N, HEAD_SIZE), half),
-        pltpu.VMEM((N * N, HEAD_SIZE), full),
+        pltpu.VMEM((HALF * N, HEAD_SIZE), full),
         pltpu.VMEM((2, 1, HEAD_SIZE), full),
         pltpu.VMEM((N, N, HEAD_SIZE), half),
         pltpu.VMEM((N, 1, HEAD_SIZE), full),
         pltpu.VMEM((HEAD_SIZE, HEAD_SIZE), full),
+        pltpu.VMEM((HEAD_SIZE, HEAD_SIZE), full),
         pltpu.VMEM((N, HEAD_SIZE), half),
         pltpu.VMEM((N, N, HEAD_SIZE), half),
         pltpu.VMEM((N * N, HEAD_SIZE), full),
@@ -418,11 +444,11 @@
         pltpu.VMEM((N, N, HEAD_SIZE), half),
         pltpu.SemaphoreType.DMA((11,)),
         pltpu.SemaphoreType.DMA((9,)),
-        pltpu.SemaphoreType.DMA((9,)),
+        pltpu.SemaphoreType.DMA((12,)),
     ]
     return pl.pallas_call(
         kernel,
-        out_shape=jax.ShapeDtypeStruct((1, STEPS, columns), half),
+        out_shape=pltpu.VMEM((1, STEPS, columns), half),
         in_specs=[smem, smem] + [hbm] * 8,
         out_specs=vmem,
         scratch_shapes=scratch,

time: 66.4 us -> 61.3 us (0.923)
  Pallas kernels: 63.6 us -> 59.3 us
  local copies, waits for them, and re-layouts: 1.28 us -> 0.6 us
    pallas_call x1, Pallas kernels: 63.6 us -> 59.3 us  [local(): pl.pallas_call(kernel, out_shape=pltpu.VMEM((1, STEPS, columns), half), i...]
    unnamed x1, local copies, waits for them, and re-layouts: 1.28 us -> 0.6 us
where the time goes in v5:
time: 61.3 us; the launch traced here: 61.2 us
  Pallas kernels  59.3 us (97%)
  between operations  1.3 us (2%)
    pallas_call x1, Pallas kernels, local(): pl.pallas_call(kernel, out_shape=pltpu.VMEM((1, STEPS, columns), half), i...  59.3 us

profile of v5, /device:TPU:1, one launch (start us, length us, event | category | flops | bytes accessed | tf_op | source)
XLA Modules:
  0.0 61.2 jit_solution(4105353882049219294)
XLA Ops:
  1.3 59.3 %decode_block.1 = bf16[1,2,1024]{2,1,0:T(2,128)(2,1)S(1)} custom-call(s32[1]{0:T(128)S(6)} %copy.13.lengths, s32[1]{0:T(128)S(6)} %copy.14.positions, bf16[16,2,1024]{2,1,0:T(2,128)(2,1)} %tokens_hbm.1, bf16[1024]{0:T(1024)(128)(2,1)} %gain_hbm.1, bf16[1024,1024]{1,0:T(8,128)(2,1)} %w_query_hbm.1, bf16[64,1024]{1,0:T(8,128)(2,1)} %bitcast.2, ...), custom_call_target="tpu_custom_call" | custom-call | tf_op jit(solution)/shard_map/decode_block/pallas_call | solution.py:449
  60.6 0.6 copy.12
